TPU v7x, 32 devices: a whole 2x2x4 slice. The times are simulated.
32 devices in a mesh: tok: 4 (over z), lat: 8 (over y, x, core).
Axes of the slice: x: 2, y: 2, z: 4, core: 2. Of those that a mesh axis runs over, the one named last changes fastest.
Arguments:
- residuals: bfloat16 [2048, 4096], P('tok', 'lat'), may hold values from -6 to 6
- dictionary: bfloat16 [16384, 4096], P('lat'), may hold values from -0.09375 to 0.09375
- enc_bias: float32 [16384], P('lat'), may hold values from -3 to 3
- dec_bias: float32 [4096], replicated, may hold values from -3 to 3
- tile_ids: int32 [16, 8, 4], P('tok', 'lat'), may hold values from 0 to 31, as said below
- tile_counts: int32 [16, 8], P('tok', 'lat'), may hold values from 0 to 4, as said below
Outputs:
- tile_codes: bfloat16 [16, 8, 4, 8192], P('tok', None, None, 'lat')
- reconstruction: bfloat16 [2048, 4096], P('tok', 'lat')
- decoder_grad: float32 [16384, 4096], P('lat', 'tok')
Inputs may be any that keep to these rules, and one draw needn't show every extreme that they name: `tile_ids`: for each token block and latent shard the 4 entries are distinct latent blocks; only the first tile_counts entries count. `tile_counts`: every draw has token blocks with all 4 slots active on every latent shard.
All inputs are finite; a program needn't handle non-finite values.
Results may differ from a plain program's by a relative error of at most 0.02.
Values may be sent and summed in bfloat16 or wider, within the bound.
A program may use at most 128 MiB of HBM per device.

v0:
```python
import jax
import jax.numpy as jnp
from jax import lax
from jax.sharding import PartitionSpec as P

TILE_ROWS = 128
LAT_TILE = 64


def body(residuals, dictionary, enc_bias, dec_bias, tile_ids, tile_counts):
    tok_rows = residuals.shape[0]
    lat_rows = dictionary.shape[0]
    model_width = dictionary.shape[1]
    blocks = tok_rows // TILE_ROWS
    lat_blocks = lat_rows // LAT_TILE
    slot_count = tile_ids.shape[2]
    gathered = lax.all_gather(residuals, "lat", axis=1, tiled=True)
    centered = (gathered.astype(jnp.float32) - dec_bias).astype(jnp.bfloat16)
    preact = (
        lax.dot_general(
            centered, dictionary, (((1,), (1,)), ((), ())), preferred_element_type=jnp.float32
        )
        + enc_bias
    )
    live_slots = lax.broadcasted_iota(jnp.int32, (blocks, slot_count), 1) < tile_counts
    block_iota = lax.broadcasted_iota(jnp.int32, (blocks, slot_count, lat_blocks), 2)
    selector = ((tile_ids[:, 0, :, None] == block_iota) & live_slots[:, :, None]).astype(
        jnp.float32
    )
    tile_active = jnp.max(selector, axis=1)
    code_four = (
        jnp.maximum(preact, 0.0).reshape(blocks, TILE_ROWS, lat_blocks, LAT_TILE)
        * tile_active[:, None, :, None]
    )
    code_values = code_four.reshape(tok_rows, lat_rows).astype(jnp.bfloat16)
    picked = lax.dot_general(
        selector.astype(jnp.bfloat16),
        code_values.reshape(blocks, TILE_ROWS, lat_blocks, LAT_TILE),
        (((2,), (2,)), ((0,), (0,))),
        preferred_element_type=jnp.float32,
    )
    tile_send = picked.reshape(blocks, 1, slot_count, TILE_ROWS * LAT_TILE).astype(jnp.bfloat16)
    tile_codes = lax.all_to_all(tile_send, "lat", split_axis=3, concat_axis=1, tiled=True)
    lat_index = lax.axis_index("lat")
    col_width = model_width // lax.axis_size("lat")
    summed = lax.psum_scatter(
        lax.dot_general(
            dictionary, code_values, (((0,), (1,)), ((), ())), preferred_element_type=jnp.float32
        ).astype(jnp.bfloat16),
        "lat",
        scatter_dimension=0,
        tiled=True,
    ).astype(jnp.float32)
    recon_part = summed.T + lax.dynamic_slice_in_dim(dec_bias, lat_index * col_width, col_width, 0)
    reconstruction = recon_part.astype(jnp.bfloat16)
    error_part = (recon_part - residuals.astype(jnp.float32)).astype(jnp.bfloat16)
    error_full = lax.all_gather(error_part, "lat", axis=1, tiled=True)
    partial_value = lax.dot_general(
        code_values, error_full, (((0,), (0,)), ((), ())), preferred_element_type=jnp.float32
    )
    partial_value = partial_value.astype(jnp.bfloat16).astype(jnp.float32)
    decoder_grad = lax.psum_scatter(
        partial_value.astype(jnp.bfloat16), "tok", scatter_dimension=1, tiled=True
    ).astype(jnp.float32)
    return (tile_codes, reconstruction, decoder_grad)


def solution(mesh):
    placed = (
        P("tok", "lat"),
        P("lat", None),
        P("lat"),
        P(),
        P("tok", "lat", None),
        P("tok", "lat"),
    )
    return jax.shard_map(
        body,
        mesh=mesh,
        in_specs=placed,
        out_specs=(P("tok", None, None, "lat"), P("tok", "lat"), P("lat", "tok")),
        check_vma=False,
    )
```

profile of v0, /device:TPU:0, one launch (start us, length us, event | category | flops | bytes accessed | tf_op | source)
XLA Modules:
  0.0 477.9 jit_solution(10716479580463791452)
XLA Ops:
  7.2 0.0 all-gather.3.cloned.1.call-start
  7.2 0.7 all-gather.3.cloned.1.call-update
  7.9 0.0 reduce-scatter.3.cloned.1.call-start
  7.9 0.7 iota_compare_fusion.1
  8.7 0.8 convert_reduce_fusion
  9.4 0.1 copy.15
  9.5 0.6 mul.14
  10.1 2.5 copy.29
  12.6 0.0 copy-start.3
  12.6 0.0 copy-start.4
  12.6 5.5 %copy.16 = f32[512,2048]{1,0:T(8,128)} copy(f32[512,2048]{0,1:T(8,128)} %bitcast.37) | data formatting | bytes 8388608 | tf_op jit(solution)/shard_map/mul | solution.py:32
  18.1 31.9 %all-gather.3.cloned.1.call-done = bf16[512,4096]{1,0:T(8,128)(2,1)} async-done(((bf16[512,512]{1,0:T(8,128)(2,1)}), bf16[512,4096]{1,0:T(8,128)(2,1)}) %all-gather.3.cloned.1.call-update) | async-done | bytes 4194320 | tf_op jit(solution)/shard_map/all_gather | solution.py:17
  50.0 0.0 copy-done.3
  50.0 0.0 copy-done.4
  50.0 14.3 %multiply_convert_fusion = bf16[512,2048]{1,0:T(8,128)(2,1)S(1)} fusion(f32[512,2048]{1,0:T(8,128)} %copy.16, bf16[2048,4096]{1,0:T(8,128)(2,1)} %param.7, bf16[512,4096]{1,0:T(8,128)(2,1)} %all-gather.3.cloned.1.call-done, f32[4096]{0:T(1024)S(1)} %copy-done.3, f32[2048]{0:T(1024)S(1)} %copy-done.4), kind=kOutput, calls=%fused_computation.6 | convolution fusion | flops 8600420352 | bytes 27287552 | tf_op jit(solution)/shard_map/dot_general | solution.py:20
  64.3 13.7 %fusion = bf16[4096,512]{0,1:T(8,128)(2,1)} fusion(bf16[512,2048]{1,0:T(8,128)(2,1)S(1)} %multiply_convert_fusion, bf16[2048,4096]{1,0:T(8,128)(2,1)} %param.7), kind=kOutput, calls=%fused_computation.3 | convolution fusion | flops 8592031744 | bytes 23068672 | tf_op jit(solution)/shard_map/dot_general | solution.py:47
  78.1 0.0 copy-start
  78.1 0.0 reduce-scatter.3.cloned.1.call-update
  78.1 0.0 all-gather.5.cloned.1.call-start
  78.1 0.1 dynamic_slice.3
  78.2 51.4 %reduce-scatter.3.cloned.1.call-done = bf16[512,512]{0,1:T(8,128)(2,1)} async-done(((bf16[4096,512]{0,1:T(8,128)(2,1)}), bf16[512,512]{0,1:T(8,128)(2,1)}) %reduce-scatter.3.cloned.1.call-update) | async-done | bytes 524304 | tf_op jit(solution)/shard_map/reduce_scatter | solution.py:46
  129.6 0.0 copy-done
  129.6 2.0 fusion.3
  131.6 0.0 all-gather.5.cloned.1.call-update
  131.6 0.2 reduce-scatter.5.cloned.1.call-start
  131.8 37.8 %all-gather.5.cloned.1.call-done = bf16[512,4096]{1,0:T(8,128)(2,1)} async-done(((bf16[512,512]{1,0:T(8,128)(2,1)}), bf16[512,4096]{1,0:T(8,128)(2,1)}) %all-gather.5.cloned.1.call-update) | async-done | bytes 4194320 | tf_op jit(solution)/shard_map/all_gather | solution.py:57
  169.7 14.6 %convolution_convert_fusion = bf16[2048,4096]{1,0:T(8,128)(2,1)} fusion(bf16[512,2048]{1,0:T(8,128)(2,1)S(1)} %multiply_convert_fusion, bf16[512,4096]{1,0:T(8,128)(2,1)} %all-gather.5.cloned.1.call-done), kind=kOutput, calls=%fused_computation | convolution fusion | flops 8598323200 | bytes 23068672 | tf_op jit(solution)/shard_map/dot_general | solution.py:58
  184.2 0.0 reduce-scatter.5.cloned.1.call-update
  184.3 5.3 %reshape.53 = bf16[4,128,32,64]{3,2,1,0:T(8,128)(2,1)} reshape(bf16[512,2048]{1,0:T(8,128)(2,1)S(1)} %multiply_convert_fusion) | data formatting | bytes 4194304 | tf_op jit(solution)/shard_map/reshape | solution.py:38
  189.6 0.0 copy-start.2
  189.6 8.1 %copy.18 = bf16[4,128,32,64]{1,2,3,0:T(8,128)(2,1)S(1)} copy(bf16[4,128,32,64]{3,2,1,0:T(8,128)(2,1)} %reshape.53) | data formatting | bytes 4194304 | tf_op jit(solution)/shard_map/reshape | solution.py:38
  197.7 0.0 copy-done.2
  197.7 0.5 convolution_convert_fusion.2
  198.1 8.4 %copy.25 = bf16[4,4,128,64]{1,0,3,2:T(4,128)(2,1)} copy(bf16[4,4,128,64]{2,1,3,0:T(4,128)(2,1)S(1)} %convolution_convert_fusion.2) | data formatting | bytes 524288 | tf_op jit(solution)/shard_map/convert_element_type | solution.py:42
  206.5 16.2 %reshape.54 = bf16[8,2,8192]{2,1,0:T(2,128)(2,1)S(1)} reshape(bf16[8192,1,4,4]{3,2,1,0:T(4,128)(2,1)} %bitcast.34) | data formatting | bytes 524288
  222.7 9.3 %all_to_all.18 = bf16[8,2,8192]{2,1,0:T(2,128)(2,1)S(1)} all-to-all(bf16[8,2,8192]{2,1,0:T(2,128)(2,1)S(1)} %reshape.54), channel_id=1, replica_groups=mesh['tok'=4,'lat'=8] {'lat'}, dimensions={0} | all-to-all | bytes 524288 | tf_op jit(solution)/shard_map/all_to_all | solution.py:43
  232.0 19.0 %reshape.55 = bf16[8192,1,4,4]{3,2,1,0:T(4,128)(2,1)} reshape(bf16[8,2,8192]{2,1,0:T(2,128)(2,1)S(1)} %all_to_all.18) | data formatting | bytes 524288
  251.1 0.0 copy-start.1
  251.1 13.0 %copy.21 = bf16[4,1,4,8,1024]{4,2,3,0,1:T(4,128)(2,1)} copy(bf16[4,1,4,8,1024]{2,0,4,3,1:T(4,128)(2,1)} %bitcast.35) | data formatting | bytes 524288 | tf_op jit(solution)/shard_map/all_to_all | solution.py:43
  264.1 0.0 copy-done.1
  264.1 0.9 bitcast_convert_fusion
  265.0 199.7 %reduce-scatter.5.cloned.1.call-done = bf16[2048,1024]{1,0:T(8,128)(2,1)} async-done(((bf16[2048,4096]{1,0:T(8,128)(2,1)}), bf16[2048,1024]{1,0:T(8,128)(2,1)}) %reduce-scatter.5.cloned.1.call-update) | async-done | bytes 4194320 | tf_op jit(solution)/shard_map/reduce_scatter | solution.py:62
  464.7 6.6 %convert_element_type.69 = f32[2048,1024]{1,0:T(8,128)} convert(bf16[2048,1024]{1,0:T(8,128)(2,1)} %reduce-scatter.5.cloned.1.call-done) | non-fusion elementwise | flops 2097152 | bytes 12582912 | tf_op jit(solution)/shard_map/convert_element_type | solution.py:64
Async XLA Ops:
  7.2 42.9 %all-gather.3.cloned.1.call-start = ((), (), s32[]{:S(2)}) async-start(), calls=%async_computation.3 | async-start | bytes 4718592 | tf_op jit(solution)/shard_map/all_gather | solution.py:17
  7.9 121.7 %reduce-scatter.3.cloned.1.call-start = ((), (), s32[]{:S(2)}) async-start(), calls=%async_computation.4 | async-start | bytes 4718592 | tf_op jit(solution)/shard_map/reduce_scatter | solution.py:46
  12.6 37.4 %copy-start.3 = (f32[4096]{0:T(1024)S(1)}, f32[4096]{0:T(1024)}, u32[]{:S(2)}) copy-start(f32[4096]{0:T(1024)} %param.9) | copy-start | bytes 49156
  12.6 37.4 %copy-start.4 = (f32[2048]{0:T(1024)S(1)}, f32[2048]{0:T(1024)}, u32[]{:S(2)}) copy-start(f32[2048]{0:T(1024)} %param.8) | copy-start | bytes 24580
  78.1 51.5 %copy-start = (bf16[512,512]{1,0:T(8,128)(2,1)S(1)}, bf16[512,512]{1,0:T(8,128)(2,1)}, u32[]{:S(2)}) copy-start(bf16[512,512]{1,0:T(8,128)(2,1)} %param.6) | copy-start | bytes 1572868
  78.1 91.6 %all-gather.5.cloned.1.call-start = ((), (), s32[]{:S(2)}) async-start(), calls=%async_computation.5 | async-start | bytes 4718592 | tf_op jit(solution)/shard_map/all_gather | solution.py:57
  131.6 333.1 %reduce-scatter.5.cloned.1.call-start = ((), (), s32[]{:S(2)}) async-start(), calls=%async_computation.6 | async-start | bytes 20971520 | tf_op jit(solution)/shard_map/reduce_scatter | solution.py:62
  189.6 8.1 %copy-start.2 = (s32[4,1,4]{2,1,0:T(1,128)S(1)}, s32[4,1,4]{2,1,0:T(1,128)}, u32[]{:S(2)}) copy-start(s32[4,1,4]{2,1,0:T(1,128)} %param.10) | copy-start | bytes 196
  251.1 13.0 %copy-start.1 = (bf16[512,512]{0,1:T(8,128)(2,1)S(1)}, bf16[512,512]{0,1:T(8,128)(2,1)}, u32[]{:S(2)}) copy-start(bf16[512,512]{0,1:T(8,128)(2,1)} %reduce-scatter.3.cloned.1.call-done) | copy-start | bytes 1572868
Sparse Core Ops, SparseCore 0:
  9.9 40.1 all-gather.2
  78.2 51.3 reduce-scatter.2
  132.2 37.4 all-gather.4
  184.4 280.2 reduce-scatter.4
where the time goes:
time: 479 us; the launch traced here: 478 us
  waiting for transfers between devices  322 us (67%)
  local copies, waits for them, and re-layouts  78.7 us (16%)
  matrix products  43 us (9%)
  between operations  13.8 us (3%)
  other arithmetic  11 us (2%)
  blocking collectives  9.35 us (2%)
    reduce_scatter x1, waiting for transfers between devices, body(): lax.psum_scatter(partial_value.astype(jnp.bfloat16), 'tok', scatter_dimen...  200 us
    reduce_scatter x1, waiting for transfers between devices, body(): lax.psum_scatter(lax.dot_general(dictionary, code_values, (((0,), (1,)),...  51.4 us
    all_gather x1, waiting for transfers between devices, body(): error_full = lax.all_gather(error_part, 'lat', axis=1, tiled=True)  37.8 us
    unnamed x13, local copies, waits for them, and re-layouts  37.7 us
    all_gather x1, waiting for transfers between devices, body(): gathered = lax.all_gather(residuals, 'lat', axis=1, tiled=True)  31.9 us
    dot_general x1, matrix products, body(): lax.dot_general(code_values, error_full, (((0,), (0,)), ((), ())), prefer...  14.6 us
    dot_general x1, matrix products, body(): lax.dot_general(centered, dictionary, (((1,), (1,)), ((), ())), preferred...  14.3 us
    dot_general x1, matrix products, body(): lax.dot_general(dictionary, code_values, (((0,), (1,)), ((), ())), prefer...  13.7 us
  transfers between devices with their start and end apart: 4, of which 4 were waited for; matrix products, arithmetic and copies ran while one was open for 17% of the time, Pallas kernels for 0%

commit v1 on v0

v1 whole, which is shorter than its diff:
```python
import functools

import jax
import jax.numpy as jnp
from jax import lax
from jax.experimental import pallas as pl
from jax.experimental.pallas import tpu as pltpu
from jax.sharding import PartitionSpec as P

TILE_ROWS = 128
LAT_TILE = 64
VMEM_BYTES = 48 * 1024 * 1024


def encode_kernel(cap, ids, counts, res_ref, dec_ref, *rest):
    w_refs, e_refs, out_ref = rest[:cap], rest[cap : 2 * cap], rest[2 * cap]
    b = pl.program_id(0)
    centered = (res_ref[...].astype(jnp.float32) - dec_ref[...]).astype(jnp.bfloat16)
    weights = jnp.concatenate([w[...] for w in w_refs], axis=0)
    preact = lax.dot_general(
        centered, weights, (((1,), (1,)), ((), ())), preferred_element_type=jnp.float32
    )
    bias = jnp.concatenate([e[0] for e in e_refs], axis=1)
    slot = lax.broadcasted_iota(jnp.int32, (1, cap * LAT_TILE), 1) // LAT_TILE
    live = (slot < counts[b]).astype(jnp.float32)
    out_ref[0] = (jnp.maximum(preact + bias, 0.0) * live).astype(jnp.bfloat16)


def encode(gathered, dictionary, enc_bias, dec_bias, ids, counts):
    tok_rows, width = gathered.shape
    blocks, cap = ids.shape
    lat_blocks = dictionary.shape[0] // LAT_TILE
    ids = ids.reshape(-1)
    bias = enc_bias.reshape(lat_blocks, 1, LAT_TILE)

    def row_spec(c):
        return pl.BlockSpec((LAT_TILE, width), lambda b, i, n: (i[b * cap + c], 0))

    def bias_spec(c):
        return pl.BlockSpec((1, 1, LAT_TILE), lambda b, i, n: (i[b * cap + c], 0, 0))

    return pl.pallas_call(
        functools.partial(encode_kernel, cap),
        out_shape=jax.ShapeDtypeStruct((blocks, TILE_ROWS, cap * LAT_TILE), jnp.bfloat16),
        grid_spec=pltpu.PrefetchScalarGridSpec(
            num_scalar_prefetch=2,
            grid=(blocks,),
            in_specs=[
                pl.BlockSpec((TILE_ROWS, width), lambda b, i, n: (b, 0)),
                pl.BlockSpec((1, width), lambda b, i, n: (0, 0)),
            ]
            + [row_spec(c) for c in range(cap)]
            + [bias_spec(c) for c in range(cap)],
            out_specs=pl.BlockSpec((1, TILE_ROWS, cap * LAT_TILE), lambda b, i, n: (b, 0, 0)),
        ),
        compiler_params=pltpu.CompilerParams(vmem_limit_bytes=VMEM_BYTES),
        name="encode",
    )(ids, counts, gathered, dec_bias.reshape(1, -1), *([dictionary] * cap), *([bias] * cap))


def decode_kernel(cap, ids, place, codes_ref, *rest):
    w_refs, out_ref = rest[:cap], rest[cap]
    weights = jnp.concatenate([w[...] for w in w_refs], axis=0)
    part = jnp.dot(codes_ref[0], weights, preferred_element_type=jnp.float32)
    out_ref[...] = part.astype(jnp.bfloat16).reshape(out_ref.shape)


def decode(codes, ids, dictionary, tok_index, width, n_tok, n_lat):
    blocks, _, depth = codes.shape
    cap = depth // LAT_TILE
    per = blocks // n_tok
    rows = per * TILE_ROWS // n_lat
    split = TILE_ROWS // rows

    def row_spec(c):
        return pl.BlockSpec((LAT_TILE, width), lambda b, i, p: (i[b * cap + c], p[0]))

    return pl.pallas_call(
        functools.partial(decode_kernel, cap),
        out_shape=jax.ShapeDtypeStruct((n_lat, n_tok, rows, width), jnp.bfloat16),
        grid_spec=pltpu.PrefetchScalarGridSpec(
            num_scalar_prefetch=2,
            grid=(blocks,),
            in_specs=[pl.BlockSpec((1, TILE_ROWS, depth), lambda b, i, p: (b, 0, 0))]
            + [row_spec(c) for c in range(cap)],
            out_specs=pl.BlockSpec(
                (split, 1, rows, width), lambda b, i, p: (b % per, b // per, 0, 0)
            ),
        ),
        compiler_params=pltpu.CompilerParams(vmem_limit_bytes=VMEM_BYTES),
        name="decode",
    )(ids.reshape(-1), tok_index.reshape(1), codes, *([dictionary] * cap))


def grad_kernel(cap, per, ids, codes_ref, err_ref, out_ref):
    blocks = codes_ref.shape[0]
    split = TILE_ROWS // err_ref.shape[2]
    cols = err_ref.shape[3]
    out_ref[...] = jnp.zeros_like(out_ref)

    @pl.loop(0, blocks)
    def _(b):
        err = err_ref[pl.ds(lax.rem(b, per) * split, split), lax.div(b, per)]
        part = lax.dot_general(
            codes_ref[b],
            err.reshape(TILE_ROWS, cols),
            (((0,), (0,)), ((), ())),
            preferred_element_type=jnp.float32,
        )
        for c in range(cap):
            at = pl.ds(pl.multiple_of(ids[b * cap + c] * LAT_TILE, LAT_TILE), LAT_TILE)
            out_ref[at, :] += part[c * LAT_TILE : (c + 1) * LAT_TILE]


def grad(codes, ids, err, lat_rows):
    blocks, _, depth = codes.shape
    cap = depth // LAT_TILE
    n_lat, n_tok, rows, width = err.shape
    cols = 256
    return pl.pallas_call(
        functools.partial(grad_kernel, cap, blocks // n_tok),
        out_shape=jax.ShapeDtypeStruct((lat_rows, width), jnp.float32),
        grid_spec=pltpu.PrefetchScalarGridSpec(
            num_scalar_prefetch=1,
            grid=(width // cols,),
            in_specs=[
                pl.BlockSpec(codes.shape, lambda j, i: (0, 0, 0)),
                pl.BlockSpec((n_lat, n_tok, rows, cols), lambda j, i: (0, 0, 0, j)),
            ],
            out_specs=pl.BlockSpec((lat_rows, cols), lambda j, i: (0, j)),
        ),
        compiler_params=pltpu.CompilerParams(vmem_limit_bytes=VMEM_BYTES),
        name="grad",
    )(ids.reshape(-1), codes, err)


def body(residuals, dictionary, enc_bias, dec_bias, tile_ids, tile_counts):
    n_tok, n_lat = lax.axis_size("tok"), lax.axis_size("lat")
    tok_index, lat_index = lax.axis_index("tok"), lax.axis_index("lat")
    tok_rows = residuals.shape[0]
    blocks, _, cap = tile_ids.shape
    width = dictionary.shape[1] // n_tok
    rows = tok_rows // n_lat
    ids = tile_ids[:, 0, :]
    ids_all = lax.all_gather(ids, "tok", axis=0, tiled=True)
    gathered = lax.all_gather(residuals, "lat", axis=1, tiled=True)
    codes = encode(gathered, dictionary, enc_bias, dec_bias, ids, tile_counts[:, 0])
    codes_all = lax.all_gather(codes, "tok", axis=0, tiled=True)
    partial_sum = decode(codes_all, ids_all, dictionary, tok_index, width, n_tok, n_lat)
    own_rows = lax.dynamic_slice_in_dim(gathered, lat_index * rows, rows, 0)
    share = lax.all_to_all(
        own_rows.reshape(rows, n_tok, width).transpose(1, 0, 2), "tok", 0, 0, tiled=True
    )
    summed = lax.psum_scatter(partial_sum, "lat", scatter_dimension=0, tiled=False)
    bias = lax.dynamic_slice_in_dim(dec_bias, tok_index * width, width, 0)
    recon = summed.astype(jnp.float32) + bias
    err = (recon - share.astype(jnp.float32)).astype(jnp.bfloat16)
    err_all = lax.all_gather(err, "lat", axis=0, tiled=False)
    decoder_grad = grad(codes_all, ids_all, err_all, dictionary.shape[0])
    back = lax.all_to_all(recon.astype(jnp.bfloat16), "tok", 0, 0, tiled=True)
    back = back.transpose(1, 0, 2).reshape(rows, n_lat, -1).transpose(1, 0, 2)
    reconstruction = lax.all_to_all(back, "lat", 0, 0, tiled=True).reshape(tok_rows, -1)
    sent = codes.reshape(blocks, n_lat, TILE_ROWS // n_lat, cap, LAT_TILE)
    sent = sent.transpose(1, 0, 3, 2, 4).reshape(n_lat, blocks, cap, -1)
    tile_codes = lax.all_to_all(sent, "lat", 0, 0, tiled=True).transpose(1, 0, 2, 3)
    return (tile_codes, reconstruction, decoder_grad)


def solution(mesh):
    placed = (
        P("tok", "lat"),
        P("lat", None),
        P("lat"),
        P(),
        P("tok", "lat", None),
        P("tok", "lat"),
    )
    return jax.shard_map(
        body,
        mesh=mesh,
        in_specs=placed,
        out_specs=(P("tok", None, None, "lat"), P("tok", "lat"), P("lat", "tok")),
        check_vma=False,
    )
```

time: 479 us -> 231 us (0.48)
  waiting for transfers between devices: 322 us -> 129 us
  local copies, waits for them, and re-layouts: 78.7 us -> 18.5 us
  matrix products: 43 us -> 0 us
  Pallas kernels: 0 us -> 36.4 us
  starting transfers between devices: 0.34 us -> 15.2 us
  other arithmetic: 11 us -> 4.29 us
    reduce_scatter x2 -> x1, waiting for transfers between devices: 251 us -> 30.8 us  [body(): lax.psum_scatter(partial_sum, 'lat', scatter_dimension=0, tiled=False)]
    all_to_all x0 -> x4, waiting for transfers between devices: none -> 43.3 us  [the longest x1 13.8 us: body(): lax.all_to_all(own_rows.reshape(rows, n_tok, width).transpose(1, 0, 2), '...]
    dot_general x4 -> x0, matrix products: 43 us -> none  [the longest x1 14.6 us: body(): lax.dot_general(code_values, error_full, (((0,), (0,)), ((), ())), prefer...]
    pallas_call x0 -> x3, Pallas kernels: none -> 36.4 us  [the longest x1 17.3 us: grad(): pl.pallas_call(functools.partial(grad_kernel, cap, blocks // n_tok), out_...]
    unnamed x13 -> x19, local copies, waits for them, and re-layouts: 37.7 us -> 11.1 us
    all_gather x1 -> x2, waiting for transfers between devices: 37.8 us -> 15 us  [the longest x1 15 us: body(): codes_all = lax.all_gather(codes, 'tok', axis=0, tiled=True)]
    all_to_all x0 -> x4, starting transfers between devices: none -> 15 us  [the longest x1 4.62 us: body(): back = lax.all_to_all(recon.astype(jnp.bfloat16), 'tok', 0, 0, tiled=True)]
    all_to_all x1 -> x0, local copies, waits for them, and re-layouts: 13 us -> none  [body(): lax.all_to_all(tile_send, 'lat', split_axis=3, concat_axis=1, tiled=True)]
  transfers between devices with their start and end apart: 4 -> 8, of which waited for: 4 -> 7; matrix products, arithmetic and copies ran while one was open for 17% -> 5% of each run, Pallas kernels for 0% -> 0%
where the time goes in v1:
time: 231 us; the launch traced here: 230 us
  waiting for transfers between devices  129 us (56%)
  Pallas kernels  36.4 us (16%)
  local copies, waits for them, and re-layouts  18.5 us (8%)
  starting transfers between devices  15.2 us (7%)
  between operations  13.9 us (6%)
  blocking collectives  12.3 us (5%)
  other arithmetic  4.29 us (2%)
    all_gather x1, waiting for transfers between devices, body(): gathered = lax.all_gather(residuals, 'lat', axis=1, tiled=True)  39.4 us
    reduce_scatter x1, waiting for transfers between devices, body(): lax.psum_scatter(partial_sum, 'lat', scatter_dimension=0, tiled=False)  30.8 us
    pallas_call x1, Pallas kernels, grad(): pl.pallas_call(functools.partial(grad_kernel, cap, blocks // n_tok), out_...  17.3 us
    all_gather x1, waiting for transfers between devices, body(): codes_all = lax.all_gather(codes, 'tok', axis=0, tiled=True)  15 us
    all_to_all x1, waiting for transfers between devices, body(): lax.all_to_all(own_rows.reshape(rows, n_tok, width).transpose(1, 0, 2), '...  13.8 us
    all_gather x1, blocking collectives, body(): ids_all = lax.all_gather(ids, 'tok', axis=0, tiled=True)  12.3 us
    pallas_call x1, Pallas kernels, decode(): pl.pallas_call(functools.partial(decode_kernel, cap), out_shape=jax.Shape...  12.1 us
    all_to_all x1, waiting for transfers between devices, body(): back = lax.all_to_all(recon.astype(jnp.bfloat16), 'tok', 0, 0, tiled=True)  12.1 us
  transfers between devices with their start and end apart: 8, of which 7 were waited for; matrix products, arithmetic and copies ran while one was open for 5% of the time, Pallas kernels for 0%

profile of v1, /device:TPU:0, one launch (start us, length us, event | category | flops | bytes accessed | tf_op | source)
XLA Modules:
  0.0 229.8 jit_solution(6872282112054314179)
XLA Ops:
  7.2 0.0 all-gather.6.cloned.1.call-start
  7.2 0.7 all-gather.6.cloned.1.call-update
  7.9 0.0 all-gather.8.cloned.1.call-start
  7.9 0.5 broadcast.7
  8.5 1.3 reduce.6
  9.8 0.1 reshape_squeeze.3.ids
  9.9 0.8 reshape.38.rest_4_.rest_5_.rest_6_.rest_7_
  10.7 39.4 %all-gather.6.cloned.1.call-done.res_ref = bf16[512,4096]{1,0:T(8,128)(2,1)} async-done(((bf16[512,512]{1,0:T(8,128)(2,1)}), bf16[512,4096]{1,0:T(8,128)(2,1)}) %all-gather.6.cloned.1.call-update) | async-done | bytes 4194320 | tf_op jit(solution)/shard_map/all_gather | solution.py:146
  50.0 2.2 copy-done.1
  52.2 0.7 copy-done.5
  53.0 0.7 copy-done.6
  53.6 7.0 %encode.1 = bf16[4,128,256]{2,1,0:T(8,128)(2,1)} custom-call(s32[16]{0:T(128)S(1)} %reshape_squeeze.3.ids, s32[4]{0:T(128)S(1)} %bitcast.24, bf16[512,4096]{1,0:T(8,128)(2,1)S(1)} %copy-done.1, f32[1,4096]{1,0:T(1,128)S(1)} %bitcast.23, bf16[2048,4096]{1,0:T(8,128)(2,1)} %rest_3_.3, bf16[2048,4096]{1,0:T(8,128)(2,1)} %rest_3_.3, bf16[2048,4096]{1,0:T(8,128)(2,1)} %rest_3_.3, ...), custom_call_target="tpu_custom_call" | custom-call | tf_op jit(solution)/shard_map/encode/pallas_call | solution.py:42
  60.6 0.0 all-gather.8.cloned.1.call-update
  60.7 0.0 reduce-scatter.2.cloned.1.call-start
  60.7 12.3 %all-gather = s32[16,1,4]{2,1,0:T(1,128)S(1)} all-gather(s32[4,1,4]{2,1,0:T(1,128)S(1)} %copy-done.7), channel_id=2, replica_groups=mesh['tok'=4,'lat'=8] {'tok'}, dimensions={0}, use_global_device_ids=true | all-gather | bytes 320 | tf_op jit(solution)/shard_map/all_gather | solution.py:145
  73.0 0.7 reduce.7
  73.7 0.1 reshape.41.ids
  73.8 15.0 %all-gather.8.cloned.1.call-done.codes_ref = bf16[16,128,256]{2,1,0:T(8,128)(2,1)} async-done(((bf16[4,128,256]{2,1,0:T(8,128)(2,1)}), bf16[16,128,256]{2,1,0:T(8,128)(2,1)}) %all-gather.8.cloned.1.call-update) | async-done | bytes 1048592 | tf_op jit(solution)/shard_map/all_gather | solution.py:148
  88.8 1.2 copy-done.2
  90.0 12.1 %decode.1 = bf16[8,4,64,1024]{3,2,1,0:T(8,128)(2,1)S(1)} custom-call(s32[64]{0:T(128)S(1)} %reshape.41.ids, s32[1]{0:T(128)} %bitcast.4.place, bf16[16,128,256]{2,1,0:T(8,128)(2,1)S(1)} %copy-done.2, bf16[2048,4096]{1,0:T(8,128)(2,1)} %rest_3_.3, bf16[2048,4096]{1,0:T(8,128)(2,1)} %rest_3_.3, bf16[2048,4096]{1,0:T(8,128)(2,1)} %rest_3_.3, ...), custom_call_target="tpu_custom_call" | custom-call | tf_op jit(solution)/shard_map/decode/pallas_call | solution.py:78
  102.1 0.0 copy-start
  102.1 2.0 copy-done
  104.1 0.0 reduce-scatter.2.cloned.1.call-update
  104.2 1.1 constant_dynamic-slice_fusion
  105.3 0.8 copy.24
  106.1 3.5 %all-to-all-start.3 = ((bf16[4,64,1024]{2,1,0:T(8,128)(2,1)}), bf16[4,64,1024]{2,1,0:T(8,128)(2,1)S(1)}, u32[]{:S(2)}, u32[]{:S(2)}) async-start(bf16[4,64,1024]{2,1,0:T(8,128)(2,1)} %bitcast.21), calls=%async_computation.4 | async-start | bytes 1048576 | tf_op jit(solution)/shard_map/all_to_all | solution.py:151
  109.6 0.0 all-gather.10.cloned.1.call-start
  109.6 0.7 dynamic_slice.6
  110.3 13.8 %all-to-all-done.3 = bf16[4,64,1024]{2,1,0:T(8,128)(2,1)S(1)} async-done(((bf16[4,64,1024]{2,1,0:T(8,128)(2,1)}), bf16[4,64,1024]{2,1,0:T(8,128)(2,1)S(1)}, u32[]{:S(2)}, u32[]{:S(2)}) %all-to-all-start.3) | async-done | bytes 524320 | tf_op jit(solution)/shard_map/all_to_all | solution.py:151
  124.2 30.8 %reduce-scatter.2.cloned.1.call-done = bf16[1,4,64,1024]{3,2,1,0:T(8,128)(2,1)} async-done(((bf16[8,4,64,1024]{3,2,1,0:T(8,128)(2,1)}), bf16[1,4,64,1024]{3,2,1,0:T(8,128)(2,1)}) %reduce-scatter.2.cloned.1.call-update) | async-done | bytes 524304 | tf_op jit(solution)/shard_map/reduce_scatter | solution.py:154
  154.9 2.3 fusion.2
  157.2 0.0 all-gather.10.cloned.1.call-update
  157.2 4.6 %all-to-all-start.1 = ((bf16[4,64,1024]{2,1,0:T(8,128)(2,1)}), bf16[4,64,1024]{2,1,0:T(8,128)(2,1)S(1)}, u32[]{:S(2)}, u32[]{:S(2)}) async-start(bf16[4,64,1024]{2,1,0:T(8,128)(2,1)} %get-tuple-element.7), calls=%async_computation.2 | async-start | bytes 1048576 | tf_op jit(solution)/shard_map/all_to_all | solution.py:160
  161.9 1.3 reshape.39
  163.2 0.1 copy.17
  163.3 1.0 reshape.40
  164.3 12.1 %all-to-all-done.1 = bf16[4,64,1024]{2,1,0:T(8,128)(2,1)S(1)} async-done(((bf16[4,64,1024]{2,1,0:T(8,128)(2,1)}), bf16[4,64,1024]{2,1,0:T(8,128)(2,1)S(1)}, u32[]{:S(2)}, u32[]{:S(2)}) %all-to-all-start.1) | async-done | bytes 524320 | tf_op jit(solution)/shard_map/all_to_all | solution.py:160
  176.4 3.4 %all-to-all-start = ((bf16[8,4,4,1024]{3,2,1,0:T(4,128)(2,1)}), bf16[8,4,4,1024]{3,2,1,0:T(4,128)(2,1)S(1)}, u32[]{:S(2)}, u32[]{:S(2)}) async-start(bf16[8,4,4,1024]{3,2,1,0:T(4,128)(2,1)} %reshape.40), calls=%async_computation | async-start | bytes 524288 | tf_op jit(solution)/shard_map/all_to_all | solution.py:165
  179.8 0.4 copy.18
  180.2 0.1 reshape.43
  180.3 0.9 copy.19
  181.3 8.5 %all-to-all-done = bf16[8,4,4,1024]{3,2,1,0:T(4,128)(2,1)S(1)} async-done(((bf16[8,4,4,1024]{3,2,1,0:T(4,128)(2,1)}), bf16[8,4,4,1024]{3,2,1,0:T(4,128)(2,1)S(1)}, u32[]{:S(2)}, u32[]{:S(2)}) %all-to-all-start) | async-done | bytes 262176 | tf_op jit(solution)/shard_map/all_to_all | solution.py:165
  189.8 3.5 %all-to-all-start.2 = ((bf16[8,64,512]{2,1,0:T(8,128)(2,1)}), bf16[8,64,512]{2,1,0:T(8,128)(2,1)S(1)}, u32[]{:S(2)}, u32[]{:S(2)}) async-start(bf16[8,64,512]{2,1,0:T(8,128)(2,1)} %copy.19), calls=%async_computation.3 | async-start | bytes 1048576 | tf_op jit(solution)/shard_map/all_to_all | solution.py:162
  193.3 0.8 copy.21
  194.1 8.9 %all-to-all-done.2 = bf16[8,64,512]{2,1,0:T(8,128)(2,1)S(1)} async-done(((bf16[8,64,512]{2,1,0:T(8,128)(2,1)}), bf16[8,64,512]{2,1,0:T(8,128)(2,1)S(1)}, u32[]{:S(2)}, u32[]{:S(2)}) %all-to-all-start.2) | async-done | bytes 524320 | tf_op jit(solution)/shard_map/all_to_all | solution.py:162
  202.9 2.2 copy-done.4
  205.1 17.3 %grad.1 = f32[2048,1024]{1,0:T(8,128)} custom-call(s32[64]{0:T(128)S(1)} %reshape.41.ids, bf16[16,128,256]{2,1,0:T(8,128)(2,1)S(1)} %copy-done.3, bf16[8,4,64,1024]{3,2,1,0:T(8,128)(2,1)S(1)} %bitcast.22), custom_call_target="tpu_custom_call" | custom-call | tf_op jit(solution)/shard_map/grad/pallas_call | solution.py:120
  222.4 0.8 copy.26
  (10 shorter events, 0.0 us)
Async XLA Ops:
  7.2 42.9 %all-gather.6.cloned.1.call-start = ((), (), s32[]{:S(2)}) async-start(), calls=%async_computation.5 | async-start | bytes 4718592 | tf_op jit(solution)/shard_map/all_gather | solution.py:146
  7.9 80.9 %all-gather.8.cloned.1.call-start = ((), (), s32[]{:S(2)}) async-start(), calls=%async_computation.6 | async-start | bytes 1310720 | tf_op jit(solution)/shard_map/all_gather | solution.py:148
  50.0 2.2 copy-start.1
  52.2 0.7 copy-start.5
  53.0 0.7 copy-start.6
  53.6 7.1 %copy-start.7 = (s32[4,1,4]{2,1,0:T(1,128)S(1)}, s32[4,1,4]{2,1,0:T(1,128)}, u32[]{:S(2)}) copy-start(s32[4,1,4]{2,1,0:T(1,128)} %param.10) | copy-start | bytes 196
  60.7 94.3 %reduce-scatter.2.cloned.1.call-start = ((), (), s32[]{:S(2)}) async-start(), calls=%async_computation.7 | async-start | bytes 4718592 | tf_op jit(solution)/shard_map/reduce_scatter | solution.py:154
  88.8 1.2 copy-start.2
  102.1 2.0 copy-start
  106.1 18.1 %all-to-all-start.3 = ((bf16[4,64,1024]{2,1,0:T(8,128)(2,1)}), bf16[4,64,1024]{2,1,0:T(8,128)(2,1)S(1)}, u32[]{:S(2)}, u32[]{:S(2)}) async-start(bf16[4,64,1024]{2,1,0:T(8,128)(2,1)} %bitcast.21), calls=%async_computation.4 | async-start | bytes 1048576 | tf_op jit(solution)/shard_map/all_to_all | solution.py:151
  109.6 93.4 %all-gather.10.cloned.1.call-start = ((), (), s32[]{:S(2)}) async-start(), calls=%async_computation.8 | async-start | bytes 4718592 | tf_op jit(solution)/shard_map/all_gather | solution.py:158
  157.2 19.1 %all-to-all-start.1 = ((bf16[4,64,1024]{2,1,0:T(8,128)(2,1)}), bf16[4,64,1024]{2,1,0:T(8,128)(2,1)S(1)}, u32[]{:S(2)}, u32[]{:S(2)}) async-start(bf16[4,64,1024]{2,1,0:T(8,128)(2,1)} %get-tuple-element.7), calls=%async_computation.2 | async-start | bytes 1048576 | tf_op jit(solution)/shard_map/all_to_all | solution.py:160
  161.9 41.1 %copy-start.3 = (bf16[16,128,256]{2,1,0:T(8,128)(2,1)S(1)}, bf16[16,128,256]{2,1,0:T(8,128)(2,1)}, u32[]{:S(2)}) copy-start(bf16[16,128,256]{2,1,0:T(8,128)(2,1)} %all-gather.8.cloned.1.call-done.codes_ref) | copy-start | bytes 3145732
  176.4 13.4 %all-to-all-start = ((bf16[8,4,4,1024]{3,2,1,0:T(4,128)(2,1)}), bf16[8,4,4,1024]{3,2,1,0:T(4,128)(2,1)S(1)}, u32[]{:S(2)}, u32[]{:S(2)}) async-start(bf16[8,4,4,1024]{3,2,1,0:T(4,128)(2,1)} %reshape.40), calls=%async_computation | async-start | bytes 524288 | tf_op jit(solution)/shard_map/all_to_all | solution.py:165
  189.8 13.2 %all-to-all-start.2 = ((bf16[8,64,512]{2,1,0:T(8,128)(2,1)}), bf16[8,64,512]{2,1,0:T(8,128)(2,1)S(1)}, u32[]{:S(2)}, u32[]{:S(2)}) async-start(bf16[8,64,512]{2,1,0:T(8,128)(2,1)} %copy.19), calls=%async_computation.3 | async-start | bytes 1048576 | tf_op jit(solution)/shard_map/all_to_all | solution.py:162
  202.9 2.2 copy-start.4
Sparse Core Ops, SparseCore 0:
  9.9 40.1 all-gather.5
  60.8 27.9 all-gather.7
  104.3 50.6 reduce-scatter.1
  157.4 39.5 all-gather.9

commit v2 on v1

--- a/solution.py
+++ b/solution.py
@@ -142,7 +142,7 @@
     width = dictionary.shape[1] // n_tok
     rows = tok_rows // n_lat
     ids = tile_ids[:, 0, :]
-    ids_all = lax.all_gather(ids, "tok", axis=0, tiled=True)
+    ids_all = lax.all_gather(tile_ids[:, 0, :], "tok", axis=0, tiled=True).reshape(-1)
     gathered = lax.all_gather(residuals, "lat", axis=1, tiled=True)
     codes = encode(gathered, dictionary, enc_bias, dec_bias, ids, tile_counts[:, 0])
     codes_all = lax.all_gather(codes, "tok", axis=0, tiled=True)
@@ -166,7 +166,342 @@
     return (tile_codes, reconstruction, decoder_grad)
 
 
+def step_kernel(
+    cap,
+    res_ref, rows_hbm, cols_hbm, enc_ref, dec_ref, live_ref,
+    codes_ref, err_ref, tc_ref, rec_ref,
+    rows_v, cols_v, gath, mine, sib_out, sib_in, fwd_x, fwd_y, dir_x, dir_y, sum_x, sum_y,
+    share, rec, rows_full,
+    rows_sem, cols_sem, g_send, g_recv, e_send, e_recv,
+    c_send, c_recv, h_send, h_recv, t_send, t_recv, s_send, s_recv, p_send, p_recv,
+    b_send, b_recv, r_send, r_recv,
+):
+    z, lat = lax.axis_index("tok"), lax.axis_index("lat")
+    core, chip = lax.rem(lat, 2), lax.div(lat, 2)
+    x, y = lax.rem(chip, 2), lax.div(chip, 2)
+
+    def flip(m):
+        yy = 1 - y if m & 4 else y
+        xx = 1 - x if m & 2 else x
+        cc = 1 - core if m & 1 else core
+        return (yy * 2 + xx) * 2 + cc
+
+    started = []
+
+    def send(src, dst, send_sem, recv_sem, **where):
+        copy = pltpu.make_async_remote_copy(
+            src_ref=src, dst_ref=dst, send_sem=send_sem, recv_sem=recv_sem,
+            device_id=where, device_id_type=pl.DeviceIdType.MESH,
+        )
+        copy.start()
+        started.append(copy)
+
+    def arrive(dst, send_sem, recv_sem):
+        pltpu.make_async_remote_copy(
+            src_ref=dst, dst_ref=dst, send_sem=send_sem, recv_sem=recv_sem,
+            device_id={"lat": flip(1)}, device_id_type=pl.DeviceIdType.MESH,
+        ).wait_recv()
+
+    load_rows = pltpu.make_async_copy(rows_hbm, rows_v, rows_sem)
+    load_rows.start()
+    load_cols = pltpu.make_async_copy(cols_hbm, cols_v, cols_sem)
+    load_cols.start()
+    barrier = pltpu.get_barrier_semaphore()
+    for m in range(1, 8):
+        pl.semaphore_signal(
+            barrier, inc=1, device_id={"lat": flip(m)}, device_id_type=pl.DeviceIdType.MESH
+        )
+    for d in range(1, 4):
+        pl.semaphore_signal(
+            barrier, inc=1, device_id={"tok": lax.rem(z + d, 4)},
+            device_id_type=pl.DeviceIdType.MESH,
+        )
+    pl.semaphore_wait(barrier, 10)
+
+    def gather_start(ref, own, i, ss, rs):
+        send(own, ref.at[lat, i], ss.at[i, 0], rs.at[i, 2], lat=flip(2))
+        send(own, ref.at[lat, i], ss.at[i, 1], rs.at[i, 4], lat=flip(4))
+        send(own, ref.at[lat, i], ss.at[i, 2], rs.at[i, 1], lat=flip(1))
+
+    def gather_near(ref, i, ss, rs):
+        at_x, at_y = ref.at[flip(2), i], ref.at[flip(4), i]
+        arrive(at_x, ss.at[i, 0], rs.at[i, 2])
+        if i % 2 == 0:
+            send(at_x, at_x, ss.at[i, 3], rs.at[i, 6], lat=flip(4))
+        send(at_x, at_x, ss.at[i, 4], rs.at[i, 3], lat=flip(1))
+        arrive(at_y, ss.at[i, 0], rs.at[i, 4])
+        if i % 2 == 1:
+            send(at_y, at_y, ss.at[i, 3], rs.at[i, 6], lat=flip(2))
+        send(at_y, at_y, ss.at[i, 5], rs.at[i, 5], lat=flip(1))
+
+    def gather_far(ref, i, ss, rs):
+        at_d = ref.at[flip(6), i]
+        arrive(at_d, ss.at[i, 0], rs.at[i, 6])
+        send(at_d, at_d, ss.at[i, 6], rs.at[i, 7], lat=flip(1))
+
+    def gather_end(ref, i, ss, rs):
+        for m in (1, 3, 5, 7):
+            arrive(ref.at[flip(m), i], ss.at[i, 0], rs.at[i, m])
+
+    for i in range(4):
+        gather_start(gath, res_ref.at[i], i, g_send, g_recv)
+    for i in range(4):
+        gath[lat, i] = res_ref[i]
+    gather_near(gath, 0, g_send, g_recv)
+    load_rows.wait()
+
+    for i in range(4):
+        if i < 3:
+            gather_near(gath, i + 1, g_send, g_recv)
+        gather_far(gath, i, g_send, g_recv)
+        gather_end(gath, i, g_send, g_recv)
+        preact = enc_ref[i]
+        for s in range(8):
+            centered = (gath[s, i].astype(jnp.float32) - dec_ref[s]).astype(jnp.bfloat16)
+            weights = rows_v[i, :, s * 512 : (s + 1) * 512]
+            preact = preact + lax.dot_general(
+                centered, weights, (((1,), (1,)), ((), ())), preferred_element_type=jnp.float32
+            )
+        codes_ref[z * 4 + i] = (jnp.maximum(preact, 0.0) * live_ref[i]).astype(jnp.bfloat16)
+        for d in range(1, 4):
+            block = codes_ref.at[z * 4 + i]
+            send(block, block, c_send.at[i, d], c_recv.at[i, d], tok=lax.rem(z + d, 4))
+
+    own_rows = pl.ds(pl.multiple_of(core * 64, 64), 64)
+    other_rows = pl.ds(pl.multiple_of((1 - core) * 64, 64), 64)
+    for d in range(1, 4):
+        to = lax.rem(z + d, 4)
+        send(
+            gath.at[pl.ds(to * 2, 2), chip, own_rows], share.at[z],
+            h_send.at[d], h_recv.at[d], tok=to,
+        )
+    for h in range(2):
+        share[z, h] = gath[z * 2 + h, chip, own_rows]
+
+    for i in range(4):
+        for d in range(1, 4):
+            src = lax.rem(z + 4 - d, 4)
+            arrive(codes_ref.at[src * 4 + i], c_send.at[i, d], c_recv.at[i, d])
+
+    load_cols.wait()
+    for r, m in enumerate((6, 2, 4, 0)):
+        to_chip = lax.div(flip(m), 2)
+
+        @pl.loop(0, 4)
+        def _(q):
+            block = q * 4 + to_chip
+            weights = cols_v[block]
+            sib_out[r, q] = jnp.dot(
+                codes_ref[block, other_rows, :], weights, preferred_element_type=jnp.float32
+            ).astype(jnp.bfloat16)
+            mine[r, q] = jnp.dot(
+                codes_ref[block, own_rows, :], weights, preferred_element_type=jnp.float32
+            ).astype(jnp.bfloat16)
+
+        send(sib_out.at[r], sib_in.at[r], s_send.at[r], s_recv.at[r], lat=flip(1))
+
+    def add(r, q, *more):
+        total = mine[r, q].astype(jnp.float32) + sib_in[r, q].astype(jnp.float32)
+        for ref in more:
+            total = total + ref.astype(jnp.float32)
+        return total
+
+    def settle(r, q, *more):
+        mine[r, q] = add(r, q, *more).astype(jnp.bfloat16)
+
+    first, second = pl.ds(0, 2), pl.ds(2, 2)
+    arrive(sib_in.at[0], s_send.at[0], s_recv.at[0])
+    for q in range(4):
+        settle(0, q)
+    send(mine.at[0, first], fwd_x, p_send.at[0], p_recv.at[0], lat=flip(2))
+    send(mine.at[0, second], fwd_y, p_send.at[1], p_recv.at[1], lat=flip(4))
+    arrive(sib_in.at[1], s_send.at[1], s_recv.at[1])
+    for q in range(2):
+        settle(1, q)
+    send(mine.at[1, first], dir_x, p_send.at[2], p_recv.at[2], lat=flip(2))
+    arrive(sib_in.at[2], s_send.at[2], s_recv.at[2])
+    for q in range(2, 4):
+        settle(2, q)
+    send(mine.at[2, second], dir_y, p_send.at[3], p_recv.at[3], lat=flip(4))
+    arrive(fwd_x, p_send.at[0], p_recv.at[0])
+    for q in range(2):
+        settle(2, q, fwd_x[q])
+    send(mine.at[2, first], sum_y, p_send.at[4], p_recv.at[4], lat=flip(4))
+    arrive(fwd_y, p_send.at[1], p_recv.at[1])
+    for q in range(2, 4):
+        settle(1, q, fwd_y[q - 2])
+    send(mine.at[1, second], sum_x, p_send.at[5], p_recv.at[5], lat=flip(2))
+    arrive(sib_in.at[3], s_send.at[3], s_recv.at[3])
+    for d in range(1, 4):
+        arrive(share.at[lax.rem(z + 4 - d, 4)], h_send.at[d], h_recv.at[d])
+
+    bias = jnp.concatenate([dec_ref[z * 2], dec_ref[z * 2 + 1]], axis=1)
+
+    def finish(q, *more):
+        recon = add(3, q, *more) + bias
+        rec[q] = recon.astype(jnp.bfloat16)
+        res = jnp.concatenate([share[q, 0], share[q, 1]], axis=1).astype(jnp.float32)
+        err_ref[lat, q] = (recon - res).astype(jnp.bfloat16)
+        gather_start(err_ref, err_ref.at[lat, q], q, e_send, e_recv)
+
+    arrive(dir_x, p_send.at[2], p_recv.at[2])
+    arrive(sum_y, p_send.at[4], p_recv.at[4])
+    for q in range(2):
+        finish(q, dir_x[q], sum_y[q])
+    arrive(dir_y, p_send.at[3], p_recv.at[3])
+    arrive(sum_x, p_send.at[5], p_recv.at[5])
+    for q in range(2, 4):
+        finish(q, dir_y[q - 2], sum_x[q - 2])
+
+    for d in range(1, 4):
+        to = lax.rem(z + d, 4)
+        send(rec.at[to], rows_full.at[z], b_send.at[d], b_recv.at[d], tok=to)
+    rows_full[z] = rec[z]
+    gather_near(err_ref, 0, e_send, e_recv)
+    gather_near(err_ref, 1, e_send, e_recv)
+    for i in range(4):
+        if i < 2:
+            gather_near(err_ref, i + 2, e_send, e_recv)
+        gather_far(err_ref, i, e_send, e_recv)
+
+    own_blocks = pl.ds(z * 4, 4)
+
+    def code_rows(owner):
+        return pl.ds(pl.multiple_of(owner * 16, 16), 16)
+
+    for m in range(1, 8):
+        to = flip(m)
+        send(
+            codes_ref.at[own_blocks, code_rows(to), :], tc_ref.at[lat],
+            t_send.at[m], t_recv.at[m], lat=to,
+        )
+    tc_ref[lat] = codes_ref[own_blocks, code_rows(lat), :]
+    for d in range(1, 4):
+        src = lax.rem(z + 4 - d, 4)
+        arrive(rows_full.at[src], b_send.at[d], b_recv.at[d])
+
+    def columns(owner):
+        return pl.ds(pl.multiple_of(lax.rem(owner, 2) * 512, 512), 512)
+
+    for m in range(1, 8):
+        to = flip(m)
+        send(
+            rows_full.at[lax.div(to, 2), :, columns(to)], rec_ref.at[lat],
+            r_send.at[m], r_recv.at[m], lat=to,
+        )
+    rec_ref[lat] = rows_full[chip, :, columns(lat)]
+    for i in range(4):
+        gather_end(err_ref, i, e_send, e_recv)
+    for m in range(1, 8):
+        arrive(tc_ref.at[flip(m)], t_send.at[m], t_recv.at[m])
+        arrive(rec_ref.at[flip(m)], r_send.at[m], r_recv.at[m])
+    for copy in started:
+        copy.wait_send()
+
+
+def select_kernel(cap, ids, ids_all, dict_hbm, rows_hbm, cols_hbm, rows_sem, cols_sem):
+    z = lax.axis_index("tok")
+    width = cols_hbm.shape[2]
+    columns = pl.ds(pl.multiple_of(z * width, width), width)
+    copies = []
+    for ref, out, sem, part in (
+        (ids, rows_hbm, rows_sem, None), (ids_all, cols_hbm, cols_sem, columns)
+    ):
+        for n in range(out.shape[0] * cap):
+            at = pl.ds(pl.multiple_of(ref[n] * LAT_TILE, LAT_TILE), LAT_TILE)
+            to = pl.ds((n % cap) * LAT_TILE, LAT_TILE)
+            src = dict_hbm.at[at] if part is None else dict_hbm.at[at, part]
+            copy = pltpu.make_async_copy(src, out.at[n // cap, to], sem.at[n])
+            copy.start()
+            copies.append(copy)
+    for copy in copies:
+        copy.wait()
+
+
+def select(ids, ids_all, dictionary, cap, width):
+    depth = cap * LAT_TILE
+    anywhere = pl.BlockSpec(memory_space=pl.ANY)
+    smem = pl.BlockSpec(memory_space=pltpu.SMEM)
+    return pl.pallas_call(
+        functools.partial(select_kernel, cap),
+        out_shape=[
+            jax.ShapeDtypeStruct((ids.size // cap, depth, dictionary.shape[1]), jnp.bfloat16),
+            jax.ShapeDtypeStruct((ids_all.size // cap, depth, width), jnp.bfloat16),
+        ],
+        in_specs=[smem, smem, anywhere],
+        out_specs=[anywhere, anywhere],
+        scratch_shapes=[
+            pltpu.SemaphoreType.DMA((ids.size,)),
+            pltpu.SemaphoreType.DMA((ids_all.size,)),
+        ],
+        name="select",
+    )(ids, ids_all, dictionary)
+
+
+def small_body(residuals, dictionary, enc_bias, dec_bias, tile_ids, tile_counts):
+    cap = tile_ids.shape[2]
+    lat_rows, model = dictionary.shape
+    ids = tile_ids.reshape(-1)
+    ids_all = lax.all_gather(tile_ids[:, 0, :], "tok", axis=0, tiled=True).reshape(-1)
+    rows_sel, cols_sel = select(ids, ids_all, dictionary, cap, 1024)
+    bias = enc_bias.reshape(-1, LAT_TILE)[ids].reshape(4, 1, cap * LAT_TILE)
+    live = jnp.arange(cap, dtype=jnp.int32)[None, :] < tile_counts
+    live = jnp.repeat(live.astype(jnp.float32), LAT_TILE, axis=1).reshape(4, 1, cap * LAT_TILE)
+    bf16, f32, dma = jnp.bfloat16, jnp.float32, pltpu.SemaphoreType.DMA
+    vmem, anywhere = pl.BlockSpec(memory_space=pltpu.VMEM), pl.BlockSpec(memory_space=pl.ANY)
+    codes_all, err_all, tiles, recon = pl.pallas_call(
+        functools.partial(step_kernel, cap),
+        out_shape=[
+            jax.ShapeDtypeStruct((16, 128, cap * LAT_TILE), bf16),
+            jax.ShapeDtypeStruct((8, 4, 64, 1024), bf16),
+            jax.ShapeDtypeStruct((8, 4, 16, cap * LAT_TILE), bf16),
+            jax.ShapeDtypeStruct((8, 64, 512), bf16),
+        ],
+        in_specs=[vmem, anywhere, anywhere, vmem, vmem, vmem],
+        out_specs=[vmem, vmem, vmem, vmem],
+        scratch_shapes=[
+            pltpu.VMEM(rows_sel.shape, bf16),
+            pltpu.VMEM(cols_sel.shape, bf16),
+            pltpu.VMEM((8, 4, 128, 512), bf16),
+            pltpu.VMEM((4, 4, 64, 1024), bf16),
+            pltpu.VMEM((4, 4, 64, 1024), bf16),
+            pltpu.VMEM((4, 4, 64, 1024), bf16),
+        ]
+        + [pltpu.VMEM((2, 64, 1024), bf16)] * 6
+        + [
+            pltpu.VMEM((4, 2, 64, 512), bf16),
+            pltpu.VMEM((4, 64, 1024), bf16),
+            pltpu.VMEM((4, 64, 1024), bf16),
+            dma, dma,
+            dma((4, 7)), dma((4, 8)), dma((4, 7)), dma((4, 8)),
+            dma((4, 4)), dma((4, 4)),
+            dma((4,)), dma((4,)),
+            dma((8,)), dma((8,)),
+            dma((4,)), dma((4,)),
+            dma((6,)), dma((6,)),
+            dma((4,)), dma((4,)),
+            dma((8,)), dma((8,)),
+        ],
+        compiler_params=pltpu.CompilerParams(
+            collective_id=0, has_side_effects=True, vmem_limit_bytes=VMEM_BYTES
+        ),
+        name="step",
+    )(
+        residuals.reshape(4, 128, 512),
+        rows_sel,
+        cols_sel,
+        bias,
+        dec_bias.reshape(8, 1, 512),
+        live,
+    )
+    decoder_grad = grad(codes_all, ids_all, err_all, lat_rows)
+    tiles = tiles.reshape(8, 4, 16, cap, LAT_TILE).transpose(1, 0, 3, 2, 4).reshape(4, 8, cap, -1)
+    return tiles, recon.reshape(512, 512), decoder_grad
+
+
 def solution(mesh):
+    sizes = dict(mesh.shape)
+    chosen = small_body if sizes == {"tok": 4, "lat": 8} else body
     placed = (
         P("tok", "lat"),
         P("lat", None),
@@ -176,7 +511,7 @@
         P("tok", "lat"),
     )
     return jax.shard_map(
-        body,
+        chosen,
         mesh=mesh,
         in_specs=placed,
         out_specs=(P("tok", None, None, "lat"), P("tok", "lat"), P("lat", "tok")),

time: 231 us -> 660 us (2.86)
  Pallas kernels: 36.4 us -> 634 us
  waiting for transfers between devices: 129 us -> 0 us
  starting transfers between devices: 15.2 us -> 0 us
  between operations: 13.9 us -> 0.7 us
  local copies, waits for them, and re-layouts: 18.5 us -> 8.43 us
    pallas_call x2, Pallas kernels: 19.1 us -> 616 us  [the longest x1 511 us: select(): pl.pallas_call(functools.partial(select_kernel, cap), out_shape=[jax.Shap...]
    all_gather x3 -> x0, waiting for transfers between devices: 54.4 us -> none  [the longest x1 39.4 us: body(): gathered = lax.all_gather(residuals, 'lat', axis=1, tiled=True)]
    all_to_all x4 -> x0, waiting for transfers between devices: 43.3 us -> none  [the longest x1 13.8 us: body(): lax.all_to_all(own_rows.reshape(rows, n_tok, width).transpose(1, 0, 2), '...]
    reduce_scatter x1 -> x0, waiting for transfers between devices: 30.8 us -> none  [body(): lax.psum_scatter(partial_sum, 'lat', scatter_dimension=0, tiled=False)]
    all_to_all x4 -> x0, starting transfers between devices: 15 us -> none  [the longest x1 4.62 us: body(): back = lax.all_to_all(recon.astype(jnp.bfloat16), 'tok', 0, 0, tiled=True)]
    unnamed x19 -> x10, local copies, waits for them, and re-layouts: 11.1 us -> 3.5 us
  transfers between devices with their start and end apart: 8 -> 0, of which waited for: 7 -> 0; matrix products, arithmetic and copies ran while one was open for 5% -> 0% of each run, Pallas kernels for 0% -> 0%
where the time goes in v2:
time: 660 us; the launch traced here: 659 us
  Pallas kernels  634 us (96%)
  blocking collectives  13.7 us (2%)
  local copies, waits for them, and re-layouts  8.43 us (1%)
    pallas_call x1, Pallas kernels, select(): pl.pallas_call(functools.partial(select_kernel, cap), out_shape=[jax.Shap...  511 us
    pallas_call x1, Pallas kernels, small_body(): pl.pallas_call(functools.partial(step_kernel, cap), out_shape=[jax.ShapeD...  105 us
    pallas_call x1, Pallas kernels, grad(): pl.pallas_call(functools.partial(grad_kernel, cap, blocks // n_tok), out_...  17.3 us
    all_gather x1, blocking collectives, small_body(): lax.all_gather(tile_ids[:, 0, :], 'tok', axis=0, tiled=True).reshape(-1)  13.7 us

profile of v2, /device:TPU:0, one launch (start us, length us, event | category | flops | bytes accessed | tf_op | source)
XLA Modules:
  0.0 659.1 jit_solution(11732601602776793563)
XLA Ops:
  0.6 0.8 reshape.67
  1.4 0.7 fusion
  2.1 0.5 broadcast.36
  2.6 1.3 reduce.8
  4.0 0.6 reshape.64.ids
  4.6 0.1 broadcast_in_dim.2
  4.7 0.1 reshape_reshape.3.live_ref
  4.7 13.7 %all-gather = s32[16,1,4]{2,1,0:T(1,128)S(1)} all-gather(s32[4,1,4]{2,1,0:T(1,128)} %param.10), channel_id=2, replica_groups=mesh['tok'=4,'lat'=8] {'tok'}, dimensions={0}, use_global_device_ids=true | all-gather | bytes 320 | tf_op jit(solution)/shard_map/all_gather | solution.py:445
  18.4 0.7 reduce.9
  19.1 0.7 reshape.65.ids_all.ids
  19.8 0.8 reshape.66
  20.5 0.6 gather_fusion
  21.1 0.1 reshape.68.enc_ref
  21.2 0.0 copy-start.1
  21.2 0.0 copy-start.2
  21.2 510.9 %select.1 = (bf16[4,256,4096]{2,1,0:T(8,128)(2,1)}, bf16[16,256,1024]{2,1,0:T(8,128)(2,1)}) custom-call(s32[16]{0:T(128)} %reshape.64.ids, s32[64]{0:T(128)} %reshape.65.ids_all.ids, bf16[2048,4096]{1,0:T(8,128)(2,1)} %dict_hbm.1), custom_call_target="tpu_custom_call" | custom-call | tf_op jit(solution)/shard_map/select/pallas_call | solution.py:425
  532.0 0.0 copy-done.1
  532.0 0.0 copy-done.2
  532.1 0.0 copy-start.3
  532.1 105.4 %step.1 = (bf16[16,128,256]{2,1,0:T(8,128)(2,1)S(1)}, bf16[8,4,64,1024]{3,2,1,0:T(8,128)(2,1)}, bf16[8,4,16,256]{3,2,1,0:T(8,128)(2,1)S(1)}, bf16[8,64,512]{2,1,0:T(8,128)(2,1)S(1)}) custom-call(bf16[4,128,512]{2,1,0:T(8,128)(2,1)S(1)} %bitcast.12, bf16[4,256,4096]{2,1,0:T(8,128)(2,1)} %get-tuple-element.9.rows_hbm, ...), custom_call_target="tpu_custom_call" | custom-call | tf_op jit(solution)/shard_map/step/pallas_call | solution.py:452
  637.5 0.2 reshape.70
  637.7 0.1 copy.11
  637.8 1.0 reshape.71
  638.8 0.0 copy-done.3
  638.8 0.0 copy-start
  638.8 2.2 copy-done
  641.0 17.3 %grad.1 = f32[2048,1024]{1,0:T(8,128)} custom-call(s32[64]{0:T(128)S(1)} %copy-done.3, bf16[16,128,256]{2,1,0:T(8,128)(2,1)S(1)} %get-tuple-element.13.codes_ref, bf16[8,4,64,1024]{3,2,1,0:T(8,128)(2,1)S(1)} %copy-done), custom_call_target="tpu_custom_call" | custom-call | tf_op jit(solution)/shard_map/grad/pallas_call | solution.py:120
  658.3 0.8 copy.13
  (2 shorter events, 0.0 us)
Async XLA Ops:
  21.2 510.9 %copy-start.1 = (bf16[512,512]{1,0:T(8,128)(2,1)S(1)}, bf16[512,512]{1,0:T(8,128)(2,1)}, u32[]{:S(2)}) copy-start(bf16[512,512]{1,0:T(8,128)(2,1)} %param.6) | copy-start | bytes 1572868
  21.2 510.9 %copy-start.2 = (f32[4096]{0:T(1024)S(1)}, f32[4096]{0:T(1024)}, u32[]{:S(2)}) copy-start(f32[4096]{0:T(1024)} %param.9) | copy-start | bytes 49156
  532.1 106.8 %copy-start.3 = (s32[64]{0:T(128)S(1)}, s32[64]{0:T(128)}, u32[]{:S(2)}) copy-start(s32[64]{0:T(128)} %reshape.65.ids_all.ids) | copy-start | bytes 772
  638.8 2.2 copy-start

commit v3 on v2

--- a/solution.py
+++ b/solution.py
@@ -399,43 +399,31 @@
         copy.wait_send()
 
 
-def select_kernel(cap, ids, ids_all, dict_hbm, rows_hbm, cols_hbm, rows_sem, cols_sem):
-    z = lax.axis_index("tok")
-    width = cols_hbm.shape[2]
-    columns = pl.ds(pl.multiple_of(z * width, width), width)
-    copies = []
-    for ref, out, sem, part in (
-        (ids, rows_hbm, rows_sem, None), (ids_all, cols_hbm, cols_sem, columns)
-    ):
-        for n in range(out.shape[0] * cap):
-            at = pl.ds(pl.multiple_of(ref[n] * LAT_TILE, LAT_TILE), LAT_TILE)
-            to = pl.ds((n % cap) * LAT_TILE, LAT_TILE)
-            src = dict_hbm.at[at] if part is None else dict_hbm.at[at, part]
-            copy = pltpu.make_async_copy(src, out.at[n // cap, to], sem.at[n])
-            copy.start()
-            copies.append(copy)
-    for copy in copies:
-        copy.wait()
-
-
-def select(ids, ids_all, dictionary, cap, width):
-    depth = cap * LAT_TILE
-    anywhere = pl.BlockSpec(memory_space=pl.ANY)
-    smem = pl.BlockSpec(memory_space=pltpu.SMEM)
+def select_kernel(ids, place, *refs):
+    out_ref = refs[-1]
+    for n, ref in enumerate(refs[:-1]):
+        at = (n * LAT_TILE) % out_ref.shape[1]
+        out_ref[n * LAT_TILE // out_ref.shape[1], at : at + LAT_TILE] = ref[...]
+
+
+def select(ids, place, dictionary, cap, group, width):
+    blocks, depth = ids.size // cap, cap * LAT_TILE
+
+    def row_spec(n):
+        return pl.BlockSpec((LAT_TILE, width), lambda b, i, p: (i[b * group * cap + n], p[0]))
+
     return pl.pallas_call(
-        functools.partial(select_kernel, cap),
-        out_shape=[
-            jax.ShapeDtypeStruct((ids.size // cap, depth, dictionary.shape[1]), jnp.bfloat16),
-            jax.ShapeDtypeStruct((ids_all.size // cap, depth, width), jnp.bfloat16),
-        ],
-        in_specs=[smem, smem, anywhere],
-        out_specs=[anywhere, anywhere],
-        scratch_shapes=[
-            pltpu.SemaphoreType.DMA((ids.size,)),
-            pltpu.SemaphoreType.DMA((ids_all.size,)),
-        ],
+        select_kernel,
+        out_shape=jax.ShapeDtypeStruct((blocks, depth, width), jnp.bfloat16),
+        grid_spec=pltpu.PrefetchScalarGridSpec(
+            num_scalar_prefetch=2,
+            grid=(blocks // group,),
+            in_specs=[row_spec(n) for n in range(group * cap)],
+            out_specs=pl.BlockSpec((group, depth, width), lambda b, i, p: (b, 0, 0)),
+        ),
+        compiler_params=pltpu.CompilerParams(vmem_limit_bytes=VMEM_BYTES),
         name="select",
-    )(ids, ids_all, dictionary)
+    )(ids, place.reshape(1), *([dictionary] * (group * cap)))
 
 
 def small_body(residuals, dictionary, enc_bias, dec_bias, tile_ids, tile_counts):
@@ -443,7 +431,8 @@
     lat_rows, model = dictionary.shape
     ids = tile_ids.reshape(-1)
     ids_all = lax.all_gather(tile_ids[:, 0, :], "tok", axis=0, tiled=True).reshape(-1)
-    rows_sel, cols_sel = select(ids, ids_all, dictionary, cap, 1024)
+    rows_sel = select(ids, jnp.zeros((), jnp.int32), dictionary, cap, 1, model)
+    cols_sel = select(ids_all, lax.axis_index("tok"), dictionary, cap, 2, 1024)
     bias = enc_bias.reshape(-1, LAT_TILE)[ids].reshape(4, 1, cap * LAT_TILE)
     live = jnp.arange(cap, dtype=jnp.int32)[None, :] < tile_counts
     live = jnp.repeat(live.astype(jnp.float32), LAT_TILE, axis=1).reshape(4, 1, cap * LAT_TILE)

time: 660 us -> 165 us (0.25)
  Pallas kernels: 634 us -> 140 us
    pallas_call x1 -> x2, Pallas kernels: 511 us -> 17.1 us  [select(): pl.pallas_call(select_kernel, out_shape=jax.ShapeDtypeStruct((blocks, dep...]
where the time goes in v3:
time: 165 us; the launch traced here: 164 us
  Pallas kernels  140 us (85%)
  blocking collectives  13.7 us (8%)
  local copies, waits for them, and re-layouts  7.33 us (4%)
  other arithmetic  2.75 us (2%)
    pallas_call x1, Pallas kernels, small_body(): pl.pallas_call(functools.partial(step_kernel, cap), out_shape=[jax.ShapeD...  105 us
    pallas_call x1, Pallas kernels, grad(): pl.pallas_call(functools.partial(grad_kernel, cap, blocks // n_tok), out_...  17.3 us
    pallas_call x2, Pallas kernels, select(): pl.pallas_call(select_kernel, out_shape=jax.ShapeDtypeStruct((blocks, dep...  17.1 us
    all_gather x1, blocking collectives, small_body(): lax.all_gather(tile_ids[:, 0, :], 'tok', axis=0, tiled=True).reshape(-1)  13.7 us
    unnamed x8, local copies, waits for them, and re-layouts  3.5 us

profile of v3, /device:TPU:0, one launch (start us, length us, event | category | flops | bytes accessed | tf_op | source)
XLA Modules:
  0.0 164.2 jit_solution(4987811254136385705)
XLA Ops:
  0.6 0.8 reshape.71
  1.4 0.7 fusion
  2.1 0.5 broadcast.36
  2.6 1.3 reduce.8
  4.0 0.1 reshape.67.ids
  4.1 0.1 broadcast_in_dim.2
  4.2 0.1 reshape_reshape.3.live_ref
  4.2 13.7 %all-gather = s32[16,1,4]{2,1,0:T(1,128)S(1)} all-gather(s32[4,1,4]{2,1,0:T(1,128)} %param.10), channel_id=2, replica_groups=mesh['tok'=4,'lat'=8] {'tok'}, dimensions={0}, use_global_device_ids=true | all-gather | bytes 320 | tf_op jit(solution)/shard_map/all_gather | solution.py:433
  17.9 0.7 reduce.9
  18.6 0.1 reshape.68.ids
  18.7 0.8 reshape.70
  19.4 0.6 gather_fusion
  20.0 0.1 reshape.72.enc_ref
  20.1 9.5 %select.3.cols_hbm = bf16[16,256,1024]{2,1,0:T(8,128)(2,1)} custom-call(s32[64]{0:T(128)S(1)} %reshape.68.ids, s32[1]{0:T(128)} %bitcast.1.place, bf16[2048,4096]{1,0:T(8,128)(2,1)} %refs_7_.1, bf16[2048,4096]{1,0:T(8,128)(2,1)} %refs_7_.1, bf16[2048,4096]{1,0:T(8,128)(2,1)} %refs_7_.1, bf16[2048,4096]{1,0:T(8,128)(2,1)} %refs_7_.1, ...), custom_call_target="tpu_custom_call" | custom-call | tf_op jit(solution)/shard_map/select/pallas_call | solution.py:415
  29.6 0.0 copy-start.1
  29.6 0.0 copy-start.2
  29.6 7.6 %select.2.rows_hbm = bf16[4,256,4096]{2,1,0:T(8,128)(2,1)} custom-call(s32[16]{0:T(128)S(1)} %reshape.67.ids, s32[1]{0:T(128)} %constant.4.clone.1.place, bf16[2048,4096]{1,0:T(8,128)(2,1)} %refs_7_.1, bf16[2048,4096]{1,0:T(8,128)(2,1)} %refs_7_.1, bf16[2048,4096]{1,0:T(8,128)(2,1)} %refs_7_.1, bf16[2048,4096]{1,0:T(8,128)(2,1)} %refs_7_.1), custom_call_target="tpu_custom_call" | custom-call | tf_op jit(solution)/shard_map/select/pallas_call | solution.py:415
  37.2 0.0 copy-done.1
  37.2 0.0 copy-done.2
  37.2 105.4 %step.1 = (bf16[16,128,256]{2,1,0:T(8,128)(2,1)S(1)}, bf16[8,4,64,1024]{3,2,1,0:T(8,128)(2,1)}, bf16[8,4,16,256]{3,2,1,0:T(8,128)(2,1)S(1)}, bf16[8,64,512]{2,1,0:T(8,128)(2,1)S(1)}) custom-call(bf16[4,128,512]{2,1,0:T(8,128)(2,1)S(1)} %bitcast.13, bf16[4,256,4096]{2,1,0:T(8,128)(2,1)} %select.2.rows_hbm, bf16[16,256,1024]{2,1,0:T(8,128)(2,1)} %select.3.cols_hbm, ...), custom_call_target="tpu_custom_call" | custom-call | tf_op jit(solution)/shard_map/step/pallas_call | solution.py:441
  142.6 0.2 reshape.74
  142.8 0.1 copy.11
  142.9 1.0 reshape.75
  143.9 0.0 copy-start
  143.9 2.2 %copy-done = bf16[8,4,64,1024]{3,2,1,0:T(8,128)(2,1)S(1)} copy-done((bf16[8,4,64,1024]{3,2,1,0:T(8,128)(2,1)S(1)}, bf16[8,4,64,1024]{3,2,1,0:T(8,128)(2,1)}, u32[]{:S(2)}) %copy-start) | copy-done | bytes 4194328
  146.1 17.3 %grad.1 = f32[2048,1024]{1,0:T(8,128)} custom-call(s32[64]{0:T(128)S(1)} %reshape.68.ids, bf16[16,128,256]{2,1,0:T(8,128)(2,1)S(1)} %get-tuple-element.9.codes_ref, bf16[8,4,64,1024]{3,2,1,0:T(8,128)(2,1)S(1)} %copy-done), custom_call_target="tpu_custom_call" | custom-call | tf_op jit(solution)/shard_map/grad/pallas_call | solution.py:120
  163.4 0.8 copy.13
  (2 shorter events, 0.0 us)
Async XLA Ops:
  29.6 7.6 %copy-start.1 = (bf16[512,512]{1,0:T(8,128)(2,1)S(1)}, bf16[512,512]{1,0:T(8,128)(2,1)}, u32[]{:S(2)}) copy-start(bf16[512,512]{1,0:T(8,128)(2,1)} %param.6) | copy-start | bytes 1572868
  29.6 7.6 %copy-start.2 = (f32[4096]{0:T(1024)S(1)}, f32[4096]{0:T(1024)}, u32[]{:S(2)}) copy-start(f32[4096]{0:T(1024)} %param.9) | copy-start | bytes 49156
  143.9 2.2 %copy-start = (bf16[8,4,64,1024]{3,2,1,0:T(8,128)(2,1)S(1)}, bf16[8,4,64,1024]{3,2,1,0:T(8,128)(2,1)}, u32[]{:S(2)}) copy-start(bf16[8,4,64,1024]{3,2,1,0:T(8,128)(2,1)} %get-tuple-element.10.err_ref) | copy-start | bytes 12582916

commit v4 on v3

--- a/solution.py
+++ b/solution.py
@@ -98,7 +98,7 @@
     cols = err_ref.shape[3]
     out_ref[...] = jnp.zeros_like(out_ref)
 
-    @pl.loop(0, blocks)
+    @pl.loop(0, blocks, unroll=4)
     def _(b):
         err = err_ref[pl.ds(lax.rem(b, per) * split, split), lax.div(b, per)]
         part = lax.dot_general(
@@ -116,7 +116,7 @@
     blocks, _, depth = codes.shape
     cap = depth // LAT_TILE
     n_lat, n_tok, rows, width = err.shape
-    cols = 256
+    cols = 512
     return pl.pallas_call(
         functools.partial(grad_kernel, cap, blocks // n_tok),
         out_shape=jax.ShapeDtypeStruct((lat_rows, width), jnp.float32),
@@ -422,6 +422,9 @@
             out_specs=pl.BlockSpec((group, depth, width), lambda b, i, p: (b, 0, 0)),
         ),
         compiler_params=pltpu.CompilerParams(vmem_limit_bytes=VMEM_BYTES),
+        cost_estimate=pl.CostEstimate(
+            flops=0, bytes_accessed=4 * blocks * depth * width, transcendentals=0
+        ),
         name="select",
     )(ids, place.reshape(1), *([dictionary] * (group * cap)))
 
@@ -430,7 +433,12 @@
     cap = tile_ids.shape[2]
     lat_rows, model = dictionary.shape
     ids = tile_ids.reshape(-1)
-    ids_all = lax.all_gather(tile_ids[:, 0, :], "tok", axis=0, tiled=True).reshape(-1)
+    pieces = [ids] + [
+        lax.ppermute(ids, "tok", [(n, (n + d) % 4) for n in range(4)]) for d in range(1, 4)
+    ]
+    group = jnp.arange(4, dtype=jnp.int32)[:, None]
+    from_group = lax.rem(lax.axis_index("tok") + 4 - group, 4)
+    ids_all = sum(jnp.where(from_group == d, pieces[d][None, :], 0) for d in range(4)).reshape(-1)
     rows_sel = select(ids, jnp.zeros((), jnp.int32), dictionary, cap, 1, model)
     cols_sel = select(ids_all, lax.axis_index("tok"), dictionary, cap, 2, 1024)
     bias = enc_bias.reshape(-1, LAT_TILE)[ids].reshape(4, 1, cap * LAT_TILE)

time: 165 us -> 148 us (0.90)
  blocking collectives: 13.7 us -> 0 us
  Pallas kernels: 140 us -> 130 us
  starting transfers between devices: 0 us -> 6.06 us
    all_gather x1 -> x0, blocking collectives: 13.7 us -> none  [small_body(): lax.all_gather(tile_ids[:, 0, :], 'tok', axis=0, tiled=True).reshape(-1)]
    pallas_call x1, Pallas kernels: 17.3 us -> 7.05 us  [grad(): pl.pallas_call(functools.partial(grad_kernel, cap, blocks // n_tok), out_...]
    ppermute x0 -> x3, starting transfers between devices: none -> 6.06 us  [small_body(): lax.ppermute(ids, 'tok', [(n, (n + d) % 4) for n in range(4)])]
  transfers between devices with their start and end apart: 0 -> 3, of which waited for: 0 -> 0; matrix products, arithmetic and copies ran while one was open for 0% -> 2% of each run, Pallas kernels for 0% -> 5%
where the time goes in v4:
time: 148 us; the launch traced here: 147 us
  Pallas kernels  130 us (88%)
  local copies, waits for them, and re-layouts  7.33 us (5%)
  starting transfers between devices  6.06 us (4%)
  other arithmetic  2.18 us (1%)
    pallas_call x1, Pallas kernels, small_body(): pl.pallas_call(functools.partial(step_kernel, cap), out_shape=[jax.ShapeD...  106 us
    pallas_call x2, Pallas kernels, select(): pl.pallas_call(select_kernel, out_shape=jax.ShapeDtypeStruct((blocks, dep...  17 us
    pallas_call x1, Pallas kernels, grad(): pl.pallas_call(functools.partial(grad_kernel, cap, blocks // n_tok), out_...  7.05 us
    ppermute x3, starting transfers between devices, small_body(): lax.ppermute(ids, 'tok', [(n, (n + d) % 4) for n in range(4)])  6.06 us
    unnamed x8, local copies, waits for them, and re-layouts  3.5 us
  transfers between devices with their start and end apart: 3, of which 0 were waited for; matrix products, arithmetic and copies ran while one was open for 2% of the time, Pallas kernels for 5%

profile of v4, /device:TPU:0, one launch (start us, length us, event | category | flops | bytes accessed | tf_op | source)
XLA Modules:
  0.0 146.7 jit_solution(13545137257084712764)
XLA Ops:
  0.6 0.5 broadcast.143
  1.1 1.3 reduce.5
  2.5 0.1 reshape.116.ids
  2.6 5.0 %collective-permute-start.2 = (s32[16]{0:T(128)S(1)}, s32[16]{0:T(128)S(1)}, u32[]{:S(2)}, u32[]{:S(2)}) collective-permute-start(s32[16]{0:T(128)S(1)} %reshape.116.ids), channel_id=1, source_target_pairs={{0,24},{8,0},{16,8},{24,16},{1,25},{9,1},{17,9},{25,17},{2,26},{10... | collective-permute-start | bytes 200 | tf_op jit(solution)/shard_map/ppermute | solution.py:437
  7.6 0.0 collective-permute-start.1
  7.6 1.0 collective-permute-start
  8.7 0.8 reshape.119
  9.4 0.7 fusion
  10.2 0.1 broadcast_in_dim.71
  10.2 0.1 reshape_reshape.3.live_ref
  10.3 0.8 reshape.118
  11.1 0.6 gather_fusion
  11.7 0.1 reshape.120.enc_ref
  11.7 7.5 %select.32.rows_hbm = bf16[4,256,4096]{2,1,0:T(8,128)(2,1)} custom-call(s32[16]{0:T(128)S(1)} %reshape.116.ids, s32[1]{0:T(128)} %constant.8.clone.1.place, bf16[2048,4096]{1,0:T(8,128)(2,1)} %refs_7_.1, bf16[2048,4096]{1,0:T(8,128)(2,1)} %refs_7_.1, bf16[2048,4096]{1,0:T(8,128)(2,1)} %refs_7_.1, bf16[2048,4096]{1,0:T(8,128)(2,1)} %refs_7_.1), custom_call_target="tpu_custom_call" | custom-call | bytes 16777216 | tf_op jit(solution)/shard_map/select/pallas_call | solution.py:415
  19.3 0.0 collective-permute-done.2
  19.3 0.0 collective-permute-done.1
  19.3 0.0 collective-permute-done
  19.3 0.1 select_add_fusion
  19.4 0.1 add.34.ids
  19.4 0.0 copy-start.1
  19.5 0.0 copy-start.2
  19.5 9.5 %select.33.cols_hbm = bf16[16,256,1024]{2,1,0:T(8,128)(2,1)} custom-call(s32[64]{0:T(128)S(1)} %add.34.ids, s32[1]{0:T(128)} %bitcast.1.place, bf16[2048,4096]{1,0:T(8,128)(2,1)} %refs_7_.1, bf16[2048,4096]{1,0:T(8,128)(2,1)} %refs_7_.1, bf16[2048,4096]{1,0:T(8,128)(2,1)} %refs_7_.1, bf16[2048,4096]{1,0:T(8,128)(2,1)} %refs_7_.1, ...), custom_call_target="tpu_custom_call" | custom-call | bytes 16777216 | tf_op jit(solution)/shard_map/select/pallas_call | solution.py:415
  28.9 0.0 copy-done.1
  28.9 0.0 copy-done.2
  28.9 106.4 %step.1 = (bf16[16,128,256]{2,1,0:T(8,128)(2,1)S(1)}, bf16[8,4,64,1024]{3,2,1,0:T(8,128)(2,1)}, bf16[8,4,16,256]{3,2,1,0:T(8,128)(2,1)S(1)}, bf16[8,64,512]{2,1,0:T(8,128)(2,1)S(1)}) custom-call(bf16[4,128,512]{2,1,0:T(8,128)(2,1)S(1)} %bitcast.13, bf16[4,256,4096]{2,1,0:T(8,128)(2,1)} %select.32.rows_hbm, bf16[16,256,1024]{2,1,0:T(8,128)(2,1)} %select.33.cols_hbm, ...), custom_call_target="tpu_custom_call" | custom-call | tf_op jit(solution)/shard_map/step/pallas_call | solution.py:449
  135.4 0.2 reshape.122
  135.6 0.1 copy.9
  135.7 1.0 reshape.123
  136.7 0.0 copy-start
  136.7 2.2 %copy-done = bf16[8,4,64,1024]{3,2,1,0:T(8,128)(2,1)S(1)} copy-done((bf16[8,4,64,1024]{3,2,1,0:T(8,128)(2,1)S(1)}, bf16[8,4,64,1024]{3,2,1,0:T(8,128)(2,1)}, u32[]{:S(2)}) %copy-start) | copy-done | bytes 4194328
  138.9 7.1 %grad.1 = f32[2048,1024]{1,0:T(8,128)} custom-call(s32[64]{0:T(128)S(1)} %add.34.ids, bf16[16,128,256]{2,1,0:T(8,128)(2,1)S(1)} %get-tuple-element.9.codes_ref, bf16[8,4,64,1024]{3,2,1,0:T(8,128)(2,1)S(1)} %copy-done), custom_call_target="tpu_custom_call" | custom-call | tf_op jit(solution)/shard_map/grad/pallas_call | solution.py:120
  145.9 0.8 copy.11
  (4 shorter events, 0.0 us)
Async XLA Ops:
  2.6 16.7 %collective-permute-start.2 = (s32[16]{0:T(128)S(1)}, s32[16]{0:T(128)S(1)}, u32[]{:S(2)}, u32[]{:S(2)}) collective-permute-start(s32[16]{0:T(128)S(1)} %reshape.116.ids), channel_id=1, source_target_pairs={{0,24},{8,0},{16,8},{24,16},{1,25},{9,1},{17,9},{25,17},{2,26},{10... | collective-permute-start | bytes 200 | tf_op jit(solution)/shard_map/ppermute | solution.py:437
  7.6 11.6 %collective-permute-start.1 = (s32[16]{0:T(128)S(1)}, s32[16]{0:T(128)S(1)}, u32[]{:S(2)}, u32[]{:S(2)}) collective-permute-start(s32[16]{0:T(128)S(1)} %reshape.116.ids), channel_id=1, source_target_pairs={{0,16},{8,24},{16,0},{24,8},{1,17},{9,25},{17,1},{25,9},{2,18},{10... | collective-permute-start | bytes 200 | tf_op jit(solution)/shard_map/ppermute | solution.py:437
  7.6 11.7 %collective-permute-start = (s32[16]{0:T(128)S(1)}, s32[16]{0:T(128)S(1)}, u32[]{:S(2)}, u32[]{:S(2)}) collective-permute-start(s32[16]{0:T(128)S(1)} %reshape.116.ids), channel_id=1, source_target_pairs={{0,8},{8,16},{16,24},{24,0},{1,9},{9,17},{17,25},{25,1},{2,10},{10... | collective-permute-start | bytes 200 | tf_op jit(solution)/shard_map/ppermute | solution.py:437
  19.4 9.5 %copy-start.1 = (bf16[512,512]{1,0:T(8,128)(2,1)S(1)}, bf16[512,512]{1,0:T(8,128)(2,1)}, u32[]{:S(2)}) copy-start(bf16[512,512]{1,0:T(8,128)(2,1)} %param.6) | copy-start | bytes 1572868
  19.5 9.5 %copy-start.2 = (f32[4096]{0:T(1024)S(1)}, f32[4096]{0:T(1024)}, u32[]{:S(2)}) copy-start(f32[4096]{0:T(1024)} %param.9) | copy-start | bytes 49156
  136.7 2.2 %copy-start = (bf16[8,4,64,1024]{3,2,1,0:T(8,128)(2,1)S(1)}, bf16[8,4,64,1024]{3,2,1,0:T(8,128)(2,1)}, u32[]{:S(2)}) copy-start(bf16[8,4,64,1024]{3,2,1,0:T(8,128)(2,1)} %get-tuple-element.10.err_ref) | copy-start | bytes 12582916

commit v5 on v4

--- a/solution.py
+++ b/solution.py
@@ -170,7 +170,7 @@
     cap,
     res_ref, rows_hbm, cols_hbm, enc_ref, dec_ref, live_ref,
     codes_ref, err_ref, tc_ref, rec_ref,
-    rows_v, cols_v, gath, mine, sib_out, sib_in, fwd_x, fwd_y, dir_x, dir_y, sum_x, sum_y,
+    rows_v, cols_v, gath, mine, sib_in, fwd_x, fwd_y, dir_x, dir_y, sum_x, sum_y,
     share, rec, rows_full,
     rows_sem, cols_sem, g_send, g_recv, e_send, e_recv,
     c_send, c_recv, h_send, h_recv, t_send, t_recv, s_send, s_recv, p_send, p_recv,
@@ -283,6 +283,18 @@
             src = lax.rem(z + 4 - d, 4)
             arrive(codes_ref.at[src * 4 + i], c_send.at[i, d], c_recv.at[i, d])
 
+    own_blocks = pl.ds(z * 4, 4)
+
+    def code_rows(owner):
+        return pl.ds(pl.multiple_of(owner * 16, 16), 16)
+
+    for m in range(1, 8):
+        to = flip(m)
+        send(
+            codes_ref.at[own_blocks, code_rows(to), :], tc_ref.at[lat],
+            t_send.at[m], t_recv.at[m], lat=to,
+        )
+    tc_ref[lat] = codes_ref[own_blocks, code_rows(lat), :]
     load_cols.wait()
     for r, m in enumerate((6, 2, 4, 0)):
         to_chip = lax.div(flip(m), 2)
@@ -291,46 +303,43 @@
         def _(q):
             block = q * 4 + to_chip
             weights = cols_v[block]
-            sib_out[r, q] = jnp.dot(
-                codes_ref[block, other_rows, :], weights, preferred_element_type=jnp.float32
+            mine[r, q] = jnp.dot(
+                codes_ref[block], weights, preferred_element_type=jnp.float32
             ).astype(jnp.bfloat16)
-            mine[r, q] = jnp.dot(
-                codes_ref[block, own_rows, :], weights, preferred_element_type=jnp.float32
-            ).astype(jnp.bfloat16)
-
-        send(sib_out.at[r], sib_in.at[r], s_send.at[r], s_recv.at[r], lat=flip(1))
+
+        send(mine.at[r, :, other_rows], sib_in.at[r], s_send.at[r], s_recv.at[r], lat=flip(1))
 
     def add(r, q, *more):
-        total = mine[r, q].astype(jnp.float32) + sib_in[r, q].astype(jnp.float32)
+        total = mine[r, q, own_rows, :].astype(jnp.float32) + sib_in[r, q].astype(jnp.float32)
         for ref in more:
             total = total + ref.astype(jnp.float32)
         return total
 
     def settle(r, q, *more):
-        mine[r, q] = add(r, q, *more).astype(jnp.bfloat16)
+        mine[r, q, own_rows, :] = add(r, q, *more).astype(jnp.bfloat16)
 
     first, second = pl.ds(0, 2), pl.ds(2, 2)
     arrive(sib_in.at[0], s_send.at[0], s_recv.at[0])
     for q in range(4):
         settle(0, q)
-    send(mine.at[0, first], fwd_x, p_send.at[0], p_recv.at[0], lat=flip(2))
-    send(mine.at[0, second], fwd_y, p_send.at[1], p_recv.at[1], lat=flip(4))
+    send(mine.at[0, first, own_rows], fwd_x, p_send.at[0], p_recv.at[0], lat=flip(2))
+    send(mine.at[0, second, own_rows], fwd_y, p_send.at[1], p_recv.at[1], lat=flip(4))
     arrive(sib_in.at[1], s_send.at[1], s_recv.at[1])
     for q in range(2):
         settle(1, q)
-    send(mine.at[1, first], dir_x, p_send.at[2], p_recv.at[2], lat=flip(2))
+    send(mine.at[1, first, own_rows], dir_x, p_send.at[2], p_recv.at[2], lat=flip(2))
     arrive(sib_in.at[2], s_send.at[2], s_recv.at[2])
     for q in range(2, 4):
         settle(2, q)
-    send(mine.at[2, second], dir_y, p_send.at[3], p_recv.at[3], lat=flip(4))
+    send(mine.at[2, second, own_rows], dir_y, p_send.at[3], p_recv.at[3], lat=flip(4))
     arrive(fwd_x, p_send.at[0], p_recv.at[0])
     for q in range(2):
         settle(2, q, fwd_x[q])
-    send(mine.at[2, first], sum_y, p_send.at[4], p_recv.at[4], lat=flip(4))
+    send(mine.at[2, first, own_rows], sum_y, p_send.at[4], p_recv.at[4], lat=flip(4))
     arrive(fwd_y, p_send.at[1], p_recv.at[1])
     for q in range(2, 4):
         settle(1, q, fwd_y[q - 2])
-    send(mine.at[1, second], sum_x, p_send.at[5], p_recv.at[5], lat=flip(2))
+    send(mine.at[1, second, own_rows], sum_x, p_send.at[5], p_recv.at[5], lat=flip(2))
     arrive(sib_in.at[3], s_send.at[3], s_recv.at[3])
     for d in range(1, 4):
         arrive(share.at[lax.rem(z + 4 - d, 4)], h_send.at[d], h_recv.at[d])
@@ -364,18 +373,6 @@
             gather_near(err_ref, i + 2, e_send, e_recv)
         gather_far(err_ref, i, e_send, e_recv)
 
-    own_blocks = pl.ds(z * 4, 4)
-
-    def code_rows(owner):
-        return pl.ds(pl.multiple_of(owner * 16, 16), 16)
-
-    for m in range(1, 8):
-        to = flip(m)
-        send(
-            codes_ref.at[own_blocks, code_rows(to), :], tc_ref.at[lat],
-            t_send.at[m], t_recv.at[m], lat=to,
-        )
-    tc_ref[lat] = codes_ref[own_blocks, code_rows(lat), :]
     for d in range(1, 4):
         src = lax.rem(z + 4 - d, 4)
         arrive(rows_full.at[src], b_send.at[d], b_recv.at[d])
@@ -460,8 +457,7 @@
             pltpu.VMEM(rows_sel.shape, bf16),
             pltpu.VMEM(cols_sel.shape, bf16),
             pltpu.VMEM((8, 4, 128, 512), bf16),
-            pltpu.VMEM((4, 4, 64, 1024), bf16),
-            pltpu.VMEM((4, 4, 64, 1024), bf16),
+            pltpu.VMEM((4, 4, 128, 1024), bf16),
             pltpu.VMEM((4, 4, 64, 1024), bf16),
         ]
         + [pltpu.VMEM((2, 64, 1024), bf16)] * 6

time: 148 us -> 145 us (0.980)
  Pallas kernels: 130 us -> 128 us
    pallas_call x1, Pallas kernels: 106 us -> 104 us  [small_body(): pl.pallas_call(functools.partial(step_kernel, cap), out_shape=[jax.ShapeD...]
where the time goes in v5:
time: 145 us; the launch traced here: 144 us
  Pallas kernels  128 us (88%)
  local copies, waits for them, and re-layouts  7.33 us (5%)
  starting transfers between devices  6.06 us (4%)
  other arithmetic  2.18 us (2%)
    pallas_call x1, Pallas kernels, small_body(): pl.pallas_call(functools.partial(step_kernel, cap), out_shape=[jax.ShapeD...  104 us
    pallas_call x2, Pallas kernels, select(): pl.pallas_call(select_kernel, out_shape=jax.ShapeDtypeStruct((blocks, dep...  17 us
    pallas_call x1, Pallas kernels, grad(): pl.pallas_call(functools.partial(grad_kernel, cap, blocks // n_tok), out_...  7.05 us
    ppermute x3, starting transfers between devices, small_body(): lax.ppermute(ids, 'tok', [(n, (n + d) % 4) for n in range(4)])  6.06 us
    unnamed x8, local copies, waits for them, and re-layouts  3.5 us
  transfers between devices with their start and end apart: 3, of which 0 were waited for; matrix products, arithmetic and copies ran while one was open for 2% of the time, Pallas kernels for 5%

profile of v5, /device:TPU:0, one launch (start us, length us, event | category | flops | bytes accessed | tf_op | source)
XLA Modules:
  0.0 143.9 jit_solution(7949342668618252070)
XLA Ops:
  0.6 0.5 broadcast.143
  1.1 1.3 reduce.5
  2.5 0.1 reshape.116.ids
  2.6 5.0 %collective-permute-start.2 = (s32[16]{0:T(128)S(1)}, s32[16]{0:T(128)S(1)}, u32[]{:S(2)}, u32[]{:S(2)}) collective-permute-start(s32[16]{0:T(128)S(1)} %reshape.116.ids), channel_id=1, source_target_pairs={{0,24},{8,0},{16,8},{24,16},{1,25},{9,1},{17,9},{25,17},{2,26},{10... | collective-permute-start | bytes 200 | tf_op jit(solution)/shard_map/ppermute | solution.py:434
  7.6 0.0 collective-permute-start.1
  7.6 1.0 collective-permute-start
  8.7 0.8 reshape.119
  9.4 0.7 fusion
  10.2 0.1 broadcast_in_dim.71
  10.2 0.1 reshape_reshape.3.live_ref
  10.3 0.8 reshape.118
  11.1 0.6 gather_fusion
  11.7 0.1 reshape.120.enc_ref
  11.7 7.5 %select.32.rows_hbm = bf16[4,256,4096]{2,1,0:T(8,128)(2,1)} custom-call(s32[16]{0:T(128)S(1)} %reshape.116.ids, s32[1]{0:T(128)} %constant.8.clone.1.place, bf16[2048,4096]{1,0:T(8,128)(2,1)} %refs_7_.1, bf16[2048,4096]{1,0:T(8,128)(2,1)} %refs_7_.1, bf16[2048,4096]{1,0:T(8,128)(2,1)} %refs_7_.1, bf16[2048,4096]{1,0:T(8,128)(2,1)} %refs_7_.1), custom_call_target="tpu_custom_call" | custom-call | bytes 16777216 | tf_op jit(solution)/shard_map/select/pallas_call | solution.py:412
  19.3 0.0 collective-permute-done.2
  19.3 0.0 collective-permute-done.1
  19.3 0.0 collective-permute-done
  19.3 0.1 select_add_fusion
  19.4 0.1 add.34.ids
  19.4 0.0 copy-start.1
  19.5 0.0 copy-start.2
  19.5 9.5 %select.33.cols_hbm = bf16[16,256,1024]{2,1,0:T(8,128)(2,1)} custom-call(s32[64]{0:T(128)S(1)} %add.34.ids, s32[1]{0:T(128)} %bitcast.1.place, bf16[2048,4096]{1,0:T(8,128)(2,1)} %refs_7_.1, bf16[2048,4096]{1,0:T(8,128)(2,1)} %refs_7_.1, bf16[2048,4096]{1,0:T(8,128)(2,1)} %refs_7_.1, bf16[2048,4096]{1,0:T(8,128)(2,1)} %refs_7_.1, ...), custom_call_target="tpu_custom_call" | custom-call | bytes 16777216 | tf_op jit(solution)/shard_map/select/pallas_call | solution.py:412
  28.9 0.0 copy-done.1
  28.9 0.0 copy-done.2
  28.9 103.6 %step.1 = (bf16[16,128,256]{2,1,0:T(8,128)(2,1)S(1)}, bf16[8,4,64,1024]{3,2,1,0:T(8,128)(2,1)}, bf16[8,4,16,256]{3,2,1,0:T(8,128)(2,1)S(1)}, bf16[8,64,512]{2,1,0:T(8,128)(2,1)S(1)}) custom-call(bf16[4,128,512]{2,1,0:T(8,128)(2,1)S(1)} %bitcast.13, bf16[4,256,4096]{2,1,0:T(8,128)(2,1)} %select.32.rows_hbm, bf16[16,256,1024]{2,1,0:T(8,128)(2,1)} %select.33.cols_hbm, ...), custom_call_target="tpu_custom_call" | custom-call | tf_op jit(solution)/shard_map/step/pallas_call | solution.py:446
  132.5 0.2 reshape.122
  132.8 0.1 copy.9
  132.9 1.0 reshape.123
  133.9 0.0 copy-start
  133.9 2.2 %copy-done = bf16[8,4,64,1024]{3,2,1,0:T(8,128)(2,1)S(1)} copy-done((bf16[8,4,64,1024]{3,2,1,0:T(8,128)(2,1)S(1)}, bf16[8,4,64,1024]{3,2,1,0:T(8,128)(2,1)}, u32[]{:S(2)}) %copy-start) | copy-done | bytes 4194328
  136.1 7.1 %grad.1 = f32[2048,1024]{1,0:T(8,128)} custom-call(s32[64]{0:T(128)S(1)} %add.34.ids, bf16[16,128,256]{2,1,0:T(8,128)(2,1)S(1)} %get-tuple-element.9.codes_ref, bf16[8,4,64,1024]{3,2,1,0:T(8,128)(2,1)S(1)} %copy-done), custom_call_target="tpu_custom_call" | custom-call | tf_op jit(solution)/shard_map/grad/pallas_call | solution.py:120
  143.1 0.8 copy.11
  (4 shorter events, 0.0 us)
Async XLA Ops:
  2.6 16.7 %collective-permute-start.2 = (s32[16]{0:T(128)S(1)}, s32[16]{0:T(128)S(1)}, u32[]{:S(2)}, u32[]{:S(2)}) collective-permute-start(s32[16]{0:T(128)S(1)} %reshape.116.ids), channel_id=1, source_target_pairs={{0,24},{8,0},{16,8},{24,16},{1,25},{9,1},{17,9},{25,17},{2,26},{10... | collective-permute-start | bytes 200 | tf_op jit(solution)/shard_map/ppermute | solution.py:434
  7.6 11.6 %collective-permute-start.1 = (s32[16]{0:T(128)S(1)}, s32[16]{0:T(128)S(1)}, u32[]{:S(2)}, u32[]{:S(2)}) collective-permute-start(s32[16]{0:T(128)S(1)} %reshape.116.ids), channel_id=1, source_target_pairs={{0,16},{8,24},{16,0},{24,8},{1,17},{9,25},{17,1},{25,9},{2,18},{10... | collective-permute-start | bytes 200 | tf_op jit(solution)/shard_map/ppermute | solution.py:434
  7.6 11.7 %collective-permute-start = (s32[16]{0:T(128)S(1)}, s32[16]{0:T(128)S(1)}, u32[]{:S(2)}, u32[]{:S(2)}) collective-permute-start(s32[16]{0:T(128)S(1)} %reshape.116.ids), channel_id=1, source_target_pairs={{0,8},{8,16},{16,24},{24,0},{1,9},{9,17},{17,25},{25,1},{2,10},{10... | collective-permute-start | bytes 200 | tf_op jit(solution)/shard_map/ppermute | solution.py:434
  19.4 9.5 %copy-start.1 = (bf16[512,512]{1,0:T(8,128)(2,1)S(1)}, bf16[512,512]{1,0:T(8,128)(2,1)}, u32[]{:S(2)}) copy-start(bf16[512,512]{1,0:T(8,128)(2,1)} %param.6) | copy-start | bytes 1572868
  19.5 9.5 %copy-start.2 = (f32[4096]{0:T(1024)S(1)}, f32[4096]{0:T(1024)}, u32[]{:S(2)}) copy-start(f32[4096]{0:T(1024)} %param.9) | copy-start | bytes 49156
  133.9 2.2 %copy-start = (bf16[8,4,64,1024]{3,2,1,0:T(8,128)(2,1)S(1)}, bf16[8,4,64,1024]{3,2,1,0:T(8,128)(2,1)}, u32[]{:S(2)}) copy-start(bf16[8,4,64,1024]{3,2,1,0:T(8,128)(2,1)} %get-tuple-element.10.err_ref) | copy-start | bytes 12582916
